TPU v7x, 256 devices: a whole 4x4x8 slice. The times are simulated.
256 devices in a mesh: fsdp: 64 (over z, y, core), tp: 4 (over x).
Axes of the slice: x: 4, y: 4, z: 8, core: 2. Of those that a mesh axis runs over, the one named last changes fastest.
Arguments:
- momentum: float32 [8192, 26624], P('fsdp', 'tp'), may hold values from -12 to 12
- gradient: bfloat16 [8192, 26624], P('fsdp', 'tp'), may hold values from -16 to 16
- right_prior: bfloat16 [4, 6656, 512], P('tp', 'fsdp'), may hold values from -0.0390625 to 0.0390625
Outputs:
- momentum_next: float32 [8192, 26624], P('fsdp', 'tp')
- update: bfloat16 [8192, 26624], P('fsdp', 'tp')
- right_next: bfloat16 [4, 6656, 512], P('tp', 'fsdp')
All inputs are finite; a program needn't handle non-finite values.
Results may differ from a plain program's by a relative error of at most 0.009.
Values may be sent and summed in bfloat16 or wider, within the bound.
A program may use at most 128 MiB of HBM per device.

v0:
```python
import math

import jax
import jax.numpy as jnp
from jax import lax
from jax.sharding import PartitionSpec as P


def local(momentum, gradient, right_prior):
    decay = 0.95
    row_count = momentum.shape[0]
    rank_width = right_prior.shape[2]
    prior_block = right_prior[0]
    blended = momentum + gradient.astype(jnp.float32)
    blend_half = blended.astype(jnp.bfloat16)
    columns = blend_half
    partial_value = jnp.dot(
        columns,
        lax.all_gather(prior_block, "fsdp", axis=0, tiled=True),
        preferred_element_type=jnp.float32,
    )
    left_factor = lax.psum(partial_value, "tp")
    gram_matrix = lax.psum(
        jnp.dot(left_factor.T, left_factor, precision=lax.Precision.HIGHEST), "fsdp"
    )
    lower = jnp.linalg.cholesky(gram_matrix)
    orthonormal = lax.linalg.triangular_solve(
        lower, left_factor, left_side=False, lower=True, transpose_a=True
    )
    ortho_half = orthonormal.astype(jnp.bfloat16)
    columns = blend_half
    right_share = lax.psum_scatter(
        lax.dot_general(
            columns, ortho_half, (((0,), (0,)), ((), ())), preferred_element_type=jnp.float32
        ),
        "fsdp",
        scatter_dimension=0,
        tiled=True,
    )
    squares = jnp.sum(right_share * right_share, axis=0)
    totals = lax.psum(squares, ("fsdp", "tp"))
    column_scale = 1.0 / jnp.sqrt(totals + 1e-06)
    right_next = (right_share * column_scale).astype(jnp.bfloat16)[None]
    rows_all = row_count * lax.axis_size("fsdp")
    cols_all = momentum.shape[1] * lax.axis_size("tp")
    magnitude = math.sqrt(rows_all * cols_all / rank_width)
    update_left = (orthonormal * column_scale * magnitude).astype(jnp.bfloat16)
    stacked = jnp.concatenate([ortho_half, update_left], axis=0)
    right_half = right_share.astype(jnp.bfloat16)
    products = lax.dot_general(
        stacked,
        lax.all_gather(right_half, "fsdp", axis=0, tiled=True),
        (((1,), (1,)), ((), ())),
        preferred_element_type=jnp.float32,
    )
    correction = products[:row_count]
    update_block = products[row_count:]
    momentum_next = blended - (1.0 - decay) * correction
    return (momentum_next, update_block.astype(jnp.bfloat16), right_next)


def solution(mesh):
    in_specs = (P("fsdp", "tp"), P("fsdp", "tp"), P("tp", "fsdp", None))
    out_specs = (P("fsdp", "tp"), P("fsdp", "tp"), P("tp", "fsdp", None))
    return jax.shard_map(local, mesh=mesh, in_specs=in_specs, out_specs=out_specs, check_vma=False)
```

profile of v0, /device:TPU:1, one launch (start us, length us, event | category | flops | bytes accessed | tf_op | source)
XLA Modules:
  0.0 850.1 jit_solution(1299981006681626947)
XLA Ops:
  7.2 0.7 all-gather.6.cloned.1.call-update
  7.9 88.5 %all-gather.6.cloned.1.call-done = bf16[1,6656,512]{2,1,0:T(8,128)(2,1)} async-done(((bf16[1,104,512]{2,1,0:T(8,128)(2,1)}), bf16[1,6656,512]{2,1,0:T(8,128)(2,1)}) %all-gather.6.cloned.1.call-update) | async-done | bytes 6815760 | tf_op jit(solution)/shard_map/all_gather | solution.py:19
  96.5 6.2 fusion
  102.8 41.0 %all-reduce.5.cloned.1.call-done = f32[128,512]{1,0:T(8,128)} async-done(((f32[128,512]{1,0:T(8,128)}), f32[128,512]{1,0:T(8,128)}) %all-reduce.5.cloned.1.call-update) | async-done | bytes 262160 | tf_op jit(solution)/shard_map/psum | solution.py:22
  143.7 3.0 fusion.45
  146.9 187.8 %all-reduce.7.cloned.1.call-done = f32[512,512]{0,1:T(8,128)} async-done(((f32[512,512]{0,1:T(8,128)}), f32[512,512]{0,1:T(8,128)}) %all-reduce.7.cloned.1.call-update) | async-done | bytes 1048592 | tf_op jit(solution)/shard_map/psum | solution.py:23
  334.7 1.6 copy.9
  336.2 1.4 fusion.4
  337.7 11.7 %cholesky.104 = f32[128,128]{1,0:T(8,128)S(1)} custom-call(f32[128,128]{1,0:T(8,128)S(1)} %cholesky.266), custom_call_target="Cholesky" | custom-call | tf_op jit(solution)/shard_map/jit(cholesky)/cholesky | solution.py:26
  349.4 9.8 %custom-call.30 = f32[1,128,128]{1,2,0:T(8,128)S(1)} custom-call(f32[1,128,128]{2,1,0:T(8,128)S(1)} %get-tuple-element.32), custom_call_target="InvertDiagBlocksLowerTriangular" | custom-call | tf_op jit(solution)/shard_map/jit(cholesky)/cholesky | solution.py:26
  359.3 1.1 cholesky.224
  360.4 1.0 constant_dynamic-update-slice_fusion.3
  361.7 11.7 %cholesky.217 = f32[128,128]{1,0:T(8,128)S(1)} custom-call(f32[128,128]{1,0:T(8,128)S(1)} %cholesky.270), custom_call_target="Cholesky" | custom-call | tf_op jit(solution)/shard_map/jit(cholesky)/cholesky | solution.py:26
  374.1 18.5 %custom-call.31 = f32[1,128,128]{1,2,0:T(8,128)S(1)} custom-call(f32[1,128,128]{2,1,0:T(8,128)S(1)} %get-tuple-element.29), custom_call_target="InvertDiagBlocksLowerTriangular" | custom-call | tf_op jit(solution)/shard_map/jit(cholesky)/cholesky | solution.py:26
  392.5 0.9 convolution_dynamic-update-slice_fusion
  393.4 1.6 convolution_subtract_fusion.1
  395.7 13.2 %cholesky.238 = f32[128,128]{1,0:T(8,128)} custom-call(f32[128,128]{1,0:T(8,128)} %cholesky.275), custom_call_target="Cholesky" | custom-call | tf_op jit(solution)/shard_map/jit(cholesky)/cholesky | solution.py:26
  408.8 1.5 select_reduce_fusion.1
  411.0 11.3 %custom-call.32 = f32[1,128,128]{1,2,0:T(8,128)} custom-call(f32[1,128,128]{2,1,0:T(8,128)} %get-tuple-element.26), custom_call_target="InvertDiagBlocksLowerTriangular" | custom-call | tf_op jit(solution)/shard_map/jit(cholesky)/cholesky | solution.py:26
  422.3 1.7 convolution_dynamic-update-slice_fusion.1
  423.9 1.4 convolution_subtract_fusion.5
  425.4 11.7 %cholesky.255 = f32[128,128]{1,0:T(8,128)S(1)} custom-call(f32[128,128]{1,0:T(8,128)S(1)} %convolution_subtract_fusion.5), custom_call_target="Cholesky" | custom-call | tf_op jit(solution)/shard_map/jit(cholesky)/cholesky | solution.py:26
  437.7 0.7 compare_reduce_fusion
  441.7 2.3 select_select_fusion
  444.0 14.0 %while.1 = (s32[]{:T(128)}, f32[512,512]{1,0:T(8,128)}, s32[4,2]{0,1:T(2,128)S(1)}, f32[4,128,128]{2,1,0:T(8,128)}, s32[]{:T(128)}) while((s32[]{:T(128)}, f32[512,512]{1,0:T(8,128)}, s32[4,2]{0,1:T(2,128)S(1)}, f32[4,128,128]{2,1,0:T(8,128)}, s32[]{:T(128)}) %tuple.32), condition=%wide.while_cond, body=%wide.while_body.sunk | while | flops 2 | bytes 132205 | solution.py:27
  444.6 2.9 bitcast_dynamic-update-slice_fusion.2
  448.1 2.9 bitcast_dynamic-update-slice_fusion.2
  451.6 2.9 bitcast_dynamic-update-slice_fusion.2
  455.1 2.8 bitcast_dynamic-update-slice_fusion.2
  458.0 40.8 %custom-call.33 = f32[4,128,128]{1,2,0:T(8,128)} custom-call(f32[4,128,128]{2,1,0:T(8,128)} %get-tuple-element.10), custom_call_target="InvertDiagBlocksLowerTriangular" | custom-call | tf_op jit(solution)/shard_map/triangular_solve | solution.py:27
  498.7 1.3 fusion.31
  500.0 1.2 convolution_subtract_fusion.3
  501.2 1.1 fusion.29
  502.3 1.3 convolution_subtract_fusion.2
  503.6 1.1 fusion.28
  504.8 1.5 convolution_subtract_fusion.4
  506.2 1.1 fusion.27
  508.7 6.9 fusion.41
  515.6 158.2 %reduce-scatter.4.cloned.1.call-done = f32[104,512]{1,0:T(8,128)} async-done(((f32[6656,512]{1,0:T(8,128)}), f32[104,512]{1,0:T(8,128)}) %reduce-scatter.4.cloned.1.call-update) | async-done | bytes 213008
  673.8 1.0 multiply_reduce_fusion
  674.7 78.3 %psum.23 = f32[512]{0:T(512)S(1)} all-reduce(f32[512]{0:T(512)S(1)} %multiply_reduce_fusion), channel_id=1, replica_groups=mesh['fsdp'=64,'tp'=4] {'fsdp','tp'}, use_global_device_ids=true, to_apply=%region_12.13 | all-reduce | flops 512 | bytes 4096 | tf_op jit(solution)/shard_map/psum | solution.py:41
  753.0 1.7 fusion.26
  754.8 1.7 multiply_convert_fusion
  756.5 77.1 %all-gather.4.cloned.1.call-done = bf16[6656,512]{1,0:T(8,128)(2,1)} async-done(((bf16[104,512]{1,0:T(8,128)(2,1)}), bf16[6656,512]{1,0:T(8,128)(2,1)}) %all-gather.4.cloned.1.call-update) | async-done | bytes 6815760 | tf_op jit(solution)/shard_map/all_gather | solution.py:52
  833.5 5.1 fusion.6
  838.6 1.4 slice.129
  840.0 0.7 copy-done.2
  840.7 2.4 fusion.2
  (44 shorter events, 7.6 us)
Async XLA Ops:
  7.2 89.3 %all-gather.6.cloned.1.call-start = ((), (), s32[]{:S(2)}) async-start(), calls=%async_computation.4 | async-start | bytes 6922240 | tf_op jit(solution)/shard_map/all_gather | solution.py:19
  7.9 135.8 %all-reduce.5.cloned.1.call-start = ((), (), s32[]{:S(2)}) async-start(), calls=%async_computation.1 | async-start | bytes 524288 | tf_op jit(solution)/shard_map/psum | solution.py:22
  102.7 231.9 %all-reduce.7.cloned.1.call-start = ((), (), s32[]{:S(2)}) async-start(), calls=%async_computation.2 | async-start | bytes 2097152 | tf_op jit(solution)/shard_map/psum | solution.py:23
  146.8 527.0 %reduce-scatter.4.cloned.1.call-start = ((), (), s32[]{:S(2)}) async-start(), calls=%async_computation.5 | async-start | bytes 13844480
  337.7 54.8 %copy-start.3 = (f32[512,512]{1,0:T(8,128)}, f32[512,512]{1,0:T(8,128)S(1)}, u32[]{:S(2)}) copy-start(f32[512,512]{1,0:T(8,128)S(1)} %fusion.4) | copy-start | bytes 3145732
  393.4 115.2 %copy-start = (f32[128,6656]{1,0:T(8,128)S(1)}, f32[128,6656]{1,0:T(8,128)}, u32[]{:S(2)}) copy-start(f32[128,6656]{1,0:T(8,128)} %param.3) | copy-start | bytes 10223620
  498.7 10.0 %copy-start.1 = (bf16[128,6656]{1,0:T(8,128)(2,1)S(1)}, bf16[128,6656]{1,0:T(8,128)(2,1)}, u32[]{:S(2)}) copy-start(bf16[128,6656]{1,0:T(8,128)(2,1)} %param.4) | copy-start | bytes 5111812
  504.8 2.6 copy-start.5
  507.4 0.6 copy-start.6
  508.0 0.7 copy-start.4
  515.6 318.0 %all-gather.4.cloned.1.call-start = ((), (), s32[]{:S(2)}) async-start(), calls=%async_computation.3 | async-start | bytes 6922240 | tf_op jit(solution)/shard_map/all_gather | solution.py:52
  838.6 2.1 copy-start.2
Sparse Core Ops, SparseCore 0:
  10.7 85.6 all-gather.5
  102.8 40.8 all-reduce.4
  148.1 186.4 all-reduce.6
  515.7 158.0 reduce-scatter.3
  754.9 78.5 all-gather.3
where the time goes:
time: 861 us; the launch traced here: 850 us
  waiting for transfers between devices  553 us (64%)
  other arithmetic  144 us (17%)
  blocking collectives  78.3 us (9%)
  matrix products  36.7 us (4%)
  local copies, waits for them, and re-layouts  20.6 us (2%)
  between operations  17 us (2%)
    psum x1, waiting for transfers between devices, local(): lax.psum(jnp.dot(left_factor.T, left_factor, precision=lax.Precision.HIGH...  188 us
    unnamed x6, waiting for transfers between devices  159 us
    another operation x14, other arithmetic, local(): lower = jnp.linalg.cholesky(gram_matrix)  92.7 us
    all_gather x1, waiting for transfers between devices, local(): lax.all_gather(prior_block, 'fsdp', axis=0, tiled=True)  88.5 us
    psum x1, blocking collectives, local(): totals = lax.psum(squares, ('fsdp', 'tp'))  78.3 us
    all_gather x1, waiting for transfers between devices, local(): lax.all_gather(right_half, 'fsdp', axis=0, tiled=True)  77.1 us
    another operation x3, other arithmetic, local(): lax.linalg.triangular_solve(lower, left_factor, left_side=False, lower=Tr...  43.1 us
    psum x1, waiting for transfers between devices, local(): left_factor = lax.psum(partial_value, 'tp')  41 us
  transfers between devices with their start and end apart: 5, of which 5 were waited for; matrix products, arithmetic and copies ran while one was open for 0% of the time, Pallas kernels for 0%

commit v1 on v0

v1 whole, which is shorter than its diff:
```python
import functools
import math

import jax
import jax.numpy as jnp
from jax import lax
from jax.experimental import pallas as pl
from jax.experimental.pallas import tpu as pltpu
from jax.sharding import PartitionSpec as P

HIGHEST = lax.Precision.HIGHEST
MESH = pl.DeviceIdType.MESH
F32 = jnp.float32
BF16 = jnp.bfloat16
VMEM_SPEC = pl.BlockSpec(memory_space=pltpu.VMEM)
VMEM_LIMIT = 60 * 1024 * 1024
BLOCK = 128
Y_CHIPS = 4


def wrap(value, size):
    return lax.rem(value + size, size)


def exact_dot(a, b, a_dim, b_dim):
    return lax.dot_general(
        a, b, (((a_dim,), (b_dim,)), ((), ())), precision=HIGHEST, preferred_element_type=F32
    )


class Place:
    def __init__(self, nz, ny, nx):
        self.nz, self.ny, self.nx = nz, ny, nx
        index = lax.axis_index("fsdp")
        self.x = lax.axis_index("tp")
        self.core = lax.rem(index, 2)
        self.y = lax.rem(lax.div(index, 2), ny)
        self.z = lax.div(index, 2 * ny)

    def device(self, z=None, y=None, core=None, x=None):
        z = self.z if z is None else z
        y = self.y if y is None else y
        core = self.core if core is None else core
        x = self.x if x is None else x
        return ((z * self.ny + y) * 2 + core, x)

    def partner(self):
        return self.device(core=1 - self.core)

    def x_peers(self):
        return [self.device(x=wrap(self.x + o, self.nx)) for o in range(1, self.nx)]

    def y_peers(self):
        return [self.device(y=wrap(self.y + o, self.ny)) for o in range(1, self.ny)]

    def z_peers(self):
        return [self.device(z=wrap(self.z + o, self.nz)) for o in range(1, self.nz)]

    def neighbours(self):
        return [
            self.device(z=wrap(self.z + 1, self.nz)),
            self.device(z=wrap(self.z + self.nz - 1, self.nz)),
            self.device(y=wrap(self.y + 1, self.ny)),
            self.device(y=wrap(self.y + self.ny - 1, self.ny)),
        ]

    def chip(self):
        return self.z * self.ny + self.y


def greet(devices):
    barrier = pltpu.get_barrier_semaphore()
    for device in devices:
        pl.semaphore_signal(barrier, inc=1, device_id=device, device_id_type=MESH)
    pl.semaphore_wait(barrier, len(devices))


def remote(src, dst, send_sem, recv_sem, device):
    return pltpu.make_async_remote_copy(
        src_ref=src, dst_ref=dst, send_sem=send_sem, recv_sem=recv_sem,
        device_id=device, device_id_type=MESH,
    )


def halves(rows, unit):
    first = -(-(rows // 2) // unit) * unit
    return ((0, first), (first, rows - first))


def gather_plane(buf, rows, na, nb, me_a, me_b, slot, device, ssem, rsem, done=None, extras=()):
    spans = halves(rows, 16)
    half_a, half_b = na // 2, nb // 2

    def piece(a, b, part):
        offset, size = (0, rows) if part is None else spans[part]
        start = pl.multiple_of(slot(a, b) * rows + offset, 16)
        return buf.at[pl.ds(start, size), :]

    def copy(key, sending):
        kind, d, step, ra = key
        sign = 1 - 2 * d
        back = step - 1 if sending else step
        if kind == 0:
            part = d if step == half_a else None
            a, b = wrap(me_a - sign * back, na), me_b
            target = device(wrap(me_a + sign, na), me_b)
            index = d * half_a + step - 1
        else:
            part = d if step == half_b else None
            a, b = wrap(me_a + ra, na), wrap(me_b - sign * back, nb)
            target = device(me_a, wrap(me_b + sign, nb))
            index = na + (d * half_b + step - 1) * na + ra
        ref = piece(a, b, part)
        return remote(ref, ref, ssem.at[index], rsem.at[index], target)

    started = []

    def start(key):
        copy(key, True).start()
        started.append(key)

    def spread(ra):
        for d in (0, 1):
            start((1, d, 1, ra))

    def finish(ra, b):
        if done is not None:
            done(slot(wrap(me_a + ra, na), b))

    for d in (0, 1):
        start((0, d, 1, 0))
    spread(0)
    finish(0, me_b)
    events = []
    for step in range(1, half_a + 1):
        for d in (0, 1):
            events.append((step, 0, d, step, 0))
    for step in range(1, half_b + 1):
        for ra in range(na):
            for d in (0, 1):
                events.append((min(ra, na - ra) + step, 1, min(ra, na - ra), ra, d, step))
    events.sort()
    landed = {}
    extras = list(extras)
    gap = max(1, len(events) // (len(extras) + 1))
    for count, event in enumerate(events):
        if event[1] == 0:
            _, _, d, step, _ = event
            sign = 1 - 2 * d
            copy((0, d, step, 0), False).wait_recv()
            if step < half_a:
                start((0, d, step + 1, 0))
                ra = (-sign * step) % na
                spread(ra)
                finish(ra, me_b)
            else:
                landed["a"] = landed.get("a", 0) + 1
                if landed["a"] == 2:
                    spread(half_a)
                    finish(half_a, me_b)
        else:
            _, _, _, ra, d, step = event
            sign = 1 - 2 * d
            copy((1, d, step, ra), False).wait_recv()
            if step < half_b:
                start((1, d, step + 1, ra))
                finish(ra, wrap(me_b - sign * step, nb))
            else:
                landed[ra] = landed.get(ra, 0) + 1
                if landed[ra] == 2:
                    finish(ra, wrap(me_b + half_b, nb))
        if extras and (count + 1) % gap == 0:
            extras.pop(0)()
    for extra in extras:
        extra()
    for key in started:
        copy(key, True).wait_send()


def reduce_ring(total, inbox, rows, n, me, order, chunk, device, ssem, rsem, base):
    spans = halves(rows, 8)
    half = n // 2
    count = len(order)

    def index(d, step, j):
        return base + (d * half + step - 1) * count + j

    def span(part):
        return (0, rows) if part is None else spans[part]

    def rows_at(dest, j, part):
        offset, size = span(part)
        return pl.ds(pl.multiple_of(chunk(dest, j) + offset, 8), size)

    def landing(d, step, j, part):
        offset, size = span(part)
        return inbox.at[index(d, step, j), pl.ds(offset, size), :]

    def copy(d, step, j):
        sign = 1 - 2 * d
        part = d if step == 1 else None
        if step == 1:
            src = total.at[rows_at(wrap(me - sign * half, n), j, part), :]
        else:
            src = landing(d, step - 1, j, part)
        i = index(d, step, j)
        return remote(src, landing(d, step, j, part), ssem.at[i], rsem.at[i], device(wrap(me - sign, n)))

    for j in order:
        for d in (0, 1):
            copy(d, 1, j).start()
    yield
    for step in range(1, half + 1):
        for j in order:
            for d in (0, 1):
                sign = 1 - 2 * d
                copy(d, step, j).wait_recv()
                if step < half:
                    dest = wrap(me - sign * (half - step), n)
                    for part in (0, 1):
                        here = landing(d, step, j, part)
                        own = total[rows_at(dest, j, part), :]
                        if step == 1 and part != d:
                            here[...] = own
                        else:
                            here[...] = here[...] + own
                    copy(d, step + 1, j).start()
                else:
                    part = d if step == 1 else None
                    own = rows_at(me, j, part)
                    total[own, :] = total[own, :] + landing(d, step, j, part)[...]
        yield
    for step in range(1, half + 1):
        for j in order:
            for d in (0, 1):
                copy(d, step, j).wait_send()


def far_first(n):
    return sorted(range(n), key=lambda j: (-min(j, n - j), j))


def reduce_plane(total, inbox_a, inbox_b, rows, na, nb, me_a, me_b, slot, device, ssem, rsem):
    order = far_first(nb)
    yield from reduce_ring(
        total, inbox_a, rows, na, me_a, order,
        lambda dest, j: slot(dest, wrap(me_b + j, nb)) * rows,
        lambda a: device(a, me_b), ssem, rsem, 0,
    )
    used = na * nb
    yield from reduce_ring(
        total, inbox_b, rows, nb, me_b, [0],
        lambda dest, j: slot(me_a, dest) * rows,
        lambda b: device(me_a, b), ssem.at[pl.ds(used, nb)], rsem.at[pl.ds(used, nb)], 0,
    )


def column_first(place):
    return dict(
        na=place.nz, nb=place.ny, me_a=place.z, me_b=place.y,
        slot=lambda a, b: a * place.ny + b,
        device=lambda a, b: place.device(z=a, y=b),
    )


def row_first(place):
    return dict(
        na=place.ny, nb=place.nz, me_a=place.y, me_b=place.z,
        slot=lambda a, b: b * place.ny + a,
        device=lambda a, b: place.device(z=b, y=a),
    )


def run_all(steps):
    for _ in steps:
        pass


def rows_of(tile, k):
    return jnp.broadcast_to(tile[k : k + 1, :], tile.shape)


def columns_of(tile, k):
    return jnp.broadcast_to(tile[:, k : k + 1], tile.shape)


def inverse_factor(block):
    count = BLOCK // 8
    d = [block[8 * i : 8 * i + 8, :] for i in range(count)]
    row = lax.broadcasted_iota(jnp.int32, (8, BLOCK), 0)
    lane = lax.broadcasted_iota(jnp.int32, (8, BLOCK), 1)
    e = [(row + 8 * i == lane).astype(F32) for i in range(count)]
    out = []
    for s in range(count):
        c = [[columns_of(d[i], 8 * s + k) for k in range(8)] for i in range(s, count)]
        pivots = jnp.zeros((8, BLOCK), F32)
        for k in range(8):
            pivot = rows_of(c[0][k], k)
            inverse = 1.0 / pivot
            pivots = jnp.where(row == k, pivot, pivots)
            d_row, e_row = rows_of(d[s], k), rows_of(e[s], k)
            later = [rows_of(c[0][q], k) for q in range(k + 1, 8)]
            for i in range(s, count):
                factor = c[i - s][k] * inverse
                if i == s:
                    factor = jnp.where(row > k, factor, 0.0)
                d[i] = d[i] - factor * d_row
                e[i] = e[i] - factor * e_row
                for q in range(k + 1, 8):
                    c[i - s][q] = c[i - s][q] - factor * later[q - k - 1]
        out.append(e[s] * lax.rsqrt(pivots))
    return jnp.concatenate(out, axis=0)


def factor_steps(a, w):
    size = a.shape[0]
    w[...] = jnp.zeros((size, size), F32)
    for o in range(0, size, BLOCK):
        end = o + BLOCK
        inverse = inverse_factor(a[o:end, o:end])
        w[o:end, o:end] = inverse
        if end < size:
            low = exact_dot(a[end:, o:end], inverse, 1, 1)
            a[end:, o:end] = low
            a[end:, end:] = a[end:, end:] - exact_dot(low, low, 1, 1)
        if o:
            through = exact_dot(a[o:end, :o], w[:o, :o], 1, 0)
            w[o:end, :o] = -exact_dot(inverse, through, 1, 0)
        yield
def left_kernel(dims, blend, prior, left, pair, mine, given, buf, partial, inbox,
                swap_send, swap_recv, keep_sem, ring_send, ring_recv, x_send, x_recv):
    place = Place(*dims)
    core, partner = place.core, place.partner()
    shard, rank = prior.shape
    half = rank // 2
    rows, columns = blend.shape
    peers = place.x_peers()
    greet([partner] + peers + place.neighbours())

    low, high = prior[:, :half].astype(F32), prior[:, half:].astype(F32)
    given[...] = jnp.where(core == 0, high, low)
    at_mine = mine.at[pl.ds(pl.multiple_of(core * shard, 8), shard), :]
    swap = remote(given, at_mine, swap_send.at[0], swap_recv.at[0], partner)
    swap.start()
    swap_blend = remote(blend, pair.at[core], swap_send.at[1], swap_recv.at[1], partner)
    swap_blend.start()
    keep = pltpu.make_async_copy(blend, pair.at[core], keep_sem)
    keep.start()
    at_mine[...] = jnp.where(core == 0, low, high)
    swap.wait_recv()
    piece = 2 * shard
    buf[pl.ds(pl.multiple_of(place.chip() * piece, 16), piece), :] = mine[...].astype(BF16)

    @pl.when(core == 0)
    def _():
        gather_plane(buf, piece, ssem=ring_send, rsem=ring_recv, **column_first(place))

    @pl.when(core == 1)
    def _():
        gather_plane(buf, piece, ssem=ring_send, rsem=ring_recv, **row_first(place))

    keep.wait()
    swap_blend.wait_recv()
    width = 1664 if columns % 1664 == 0 else BLOCK
    partial[...] = jnp.zeros_like(partial)

    @pl.loop(0, columns // width)
    def _(i):
        at = pl.ds(pl.multiple_of(i * width, BLOCK), width)
        for c in range(2):
            own = slice(c * rows, (c + 1) * rows)
            partial[own, :] += jnp.dot(pair[c, :, at], buf[at, :], preferred_element_type=F32)

    part = 2 * rows // place.nx
    at_x = lambda x: pl.ds(pl.multiple_of(x * part, 8), part)
    copies = []
    for o, peer in enumerate(peers, 1):
        copies.append(remote(partial.at[at_x(wrap(place.x + o, place.nx)), :], inbox.at[o],
                             x_send.at[o], x_recv.at[o], peer))
        copies[-1].start()
    total = partial[at_x(place.x), :]
    for o, copy in enumerate(copies, 1):
        copy.wait_recv()
        total = total + inbox[o]
    left[at_x(place.x), :] = total
    for o, peer in enumerate(peers, 1):
        here = left.at[at_x(place.x), :]
        copies.append(remote(here, here, x_send.at[place.nx + o], x_recv.at[place.nx + o], peer))
        copies[-1].start()
    for o in range(1, place.nx):
        there = left.at[at_x(wrap(place.x - o, place.nx)), :]
        remote(there, there, x_send.at[place.nx + o], x_recv.at[place.nx + o], peers[o - 1]).wait_recv()
    for copy in copies + [swap, swap_blend]:
        copy.wait_send()


def left_factor_call(dims, blend, prior):
    nz, ny, nx = dims
    shard, rank = prior.shape
    rows, columns = blend.shape
    half = rank // 2
    ring = nz * ny + max(nz, ny)
    dma = pltpu.SemaphoreType.DMA
    return pl.pallas_call(
        functools.partial(left_kernel, dims),
        out_shape=(
            jax.ShapeDtypeStruct((2 * rows, half), F32),
            jax.ShapeDtypeStruct((2, rows, columns), BF16),
        ),
        in_specs=[VMEM_SPEC] * 2,
        out_specs=(VMEM_SPEC,) * 2,
        scratch_shapes=[
            pltpu.VMEM((2 * shard, half), F32),
            pltpu.VMEM((shard, half), F32),
            pltpu.VMEM((columns, half), BF16),
            pltpu.VMEM((2 * rows, half), F32),
            pltpu.VMEM((nx, 2 * rows // nx, half), F32),
            dma((2,)), dma((2,)), dma, dma((ring,)), dma((ring,)), dma((2 * nx,)), dma((2 * nx,)),
        ],
        compiler_params=pltpu.CompilerParams(
            collective_id=0, has_side_effects=True, vmem_limit_bytes=VMEM_LIMIT
        ),
        name="left_factor",
    )(blend, prior)


def gram_steps(place, left, both, part, z_in, y_in, gram, send, recv):
    core, partner = place.core, place.partner()
    nz, ny, nx = place.nz, place.ny, place.nx
    half = left.shape[1]
    across = 2 * half // nx
    rows = across // nz
    base = [0]

    def sems(count):
        base[0] += count
        return base[0] - count

    sent = []

    def start(src, dst, index, device):
        copy = remote(src, dst, send.at[index], recv.at[index], device)
        copy.start()
        sent.append(copy)
        return copy

    def wait(ref, index, device):
        remote(ref, ref, send.at[index], recv.at[index], device).wait_recv()

    i = sems(1)
    start(left, both.at[core], i, partner)
    both[core] = left[...]
    wait(both.at[1 - core], i, partner)
    per = half // across
    block = both[lax.div(place.x, per), :, pl.ds(pl.multiple_of(lax.rem(place.x, per) * across, BLOCK), across)]
    part[...] = exact_dot(block, left[...], 0, 0)

    z_peers, y_peers, x_peers = place.z_peers(), place.y_peers(), place.x_peers()
    at_z = lambda z: pl.ds(pl.multiple_of(z * rows, 8), rows)
    i = sems(nz)
    for o, peer in enumerate(z_peers, 1):
        start(part.at[at_z(wrap(place.z + o, nz)), :], z_in.at[o], i + o, peer)
    total = part[at_z(place.z), :]
    for o, peer in enumerate(z_peers, 1):
        wait(z_in.at[o], i + o, peer)
        total = total + z_in[o]
    i = sems(ny)
    y_in[place.y] = total
    for o, peer in enumerate(y_peers, 1):
        start(y_in.at[place.y], y_in.at[place.y], i + o, peer)
    for o, peer in enumerate(y_peers, 1):
        wait(y_in.at[wrap(place.y - o, ny)], i + o, peer)
    total = y_in[0]
    for y in range(1, ny):
        total = total + y_in[y]

    def at(x, z):
        return gram.at[core, pl.ds(pl.multiple_of(x * across + z * rows, 8), rows), :]

    at(place.x, place.z)[...] = total
    i = sems(nz)
    for o, peer in enumerate(z_peers, 1):
        start(at(place.x, place.z), at(place.x, place.z), i + o, peer)
    for o, peer in enumerate(z_peers, 1):
        wait(at(place.x, wrap(place.z - o, nz)), i + o, peer)
    whole = lambda x: gram.at[core, pl.ds(pl.multiple_of(x * across, 8), across), :]
    i = sems(nx)
    for o, peer in enumerate(x_peers, 1):
        start(whole(place.x), whole(place.x), i + o, peer)
    for o, peer in enumerate(x_peers, 1):
        wait(whole(wrap(place.x - o, nx)), i + o, peer)
    i = sems(1)
    start(gram.at[core], gram.at[core], i, partner)
    wait(gram.at[1 - core], i, partner)
    for copy in sent:
        copy.wait_send()


def gram_kernel(dims, left, gram_out, left_out, both, part, z_in, y_in, gram, send, recv):
    place = Place(*dims)
    greet([place.partner()] + place.x_peers() + place.y_peers() + place.z_peers())
    gram_steps(place, left, both, part, z_in, y_in, gram, send, recv)
    half = left.shape[1]
    rows = left.shape[0] // 2
    own = pl.ds(pl.multiple_of(place.core * rows, 8), rows)
    for c in range(2):
        gram_out[:, c * half : (c + 1) * half] = gram[c]
        left_out[:, c * half : (c + 1) * half] = both[c, own, :]


def gram_call(dims, left):
    nz, ny, nx = dims
    rows, half = left.shape
    rank = 2 * half
    across = rank // nx
    sems = 2 + 2 * nz + ny + nx
    return pl.pallas_call(
        functools.partial(gram_kernel, dims),
        out_shape=(
            jax.ShapeDtypeStruct((rank, rank), F32),
            jax.ShapeDtypeStruct((rows // 2, rank), F32),
        ),
        in_specs=[VMEM_SPEC],
        out_specs=(VMEM_SPEC,) * 2,
        scratch_shapes=[
            pltpu.VMEM((2, rows, half), F32),
            pltpu.VMEM((across, half), F32),
            pltpu.VMEM((nz, across // nz, half), F32),
            pltpu.VMEM((ny, across // nz, half), F32),
            pltpu.VMEM((2, rank, half), F32),
            pltpu.SemaphoreType.DMA((sems,)),
            pltpu.SemaphoreType.DMA((sems,)),
        ],
        compiler_params=pltpu.CompilerParams(
            collective_id=1, has_side_effects=True, vmem_limit_bytes=VMEM_LIMIT
        ),
        name="gram",
    )(left)


def factor_kernel(gram, left, w, ortho, a):
    a[...] = gram[...]
    run_all(factor_steps(a, w))
    ortho[...] = exact_dot(left[...], w[...], 1, 1)


def factor_call(gram, left):
    rank = gram.shape[0]
    return pl.pallas_call(
        factor_kernel,
        out_shape=(
            jax.ShapeDtypeStruct((rank, rank), F32),
            jax.ShapeDtypeStruct(left.shape, F32),
        ),
        in_specs=[VMEM_SPEC] * 2,
        out_specs=(VMEM_SPEC,) * 2,
        scratch_shapes=[pltpu.VMEM((rank, rank), F32)],
        compiler_params=pltpu.CompilerParams(vmem_limit_bytes=VMEM_LIMIT),
        name="factor",
    )(gram, left)


def project(pair, left, total):
    columns = pair.shape[2]
    half = left.shape[1]
    upper = left[...].astype(BF16)
    lower = (left[...] - upper.astype(F32)).astype(BF16)
    both = jnp.concatenate([upper, lower], axis=1)
    rows = pair.shape[1]
    width = 512 if columns % 512 == 0 else BLOCK

    @pl.loop(0, columns // width)
    def _(i):
        at = pl.ds(pl.multiple_of(i * width, BLOCK), width)
        value = sum(
            lax.dot_general(pair[c, :, at], both[c * rows : (c + 1) * rows], (((0,), (0,)), ((), ())),
                            preferred_element_type=F32)
            for c in range(2)
        )
        total[at, :] = value[:, :half] + value[:, half:]


def right_kernel(dims, pair, left, w, right, right_half, squares, total, inbox_a, inbox_b, both,
                 ring_send, ring_recv, swap_send, swap_recv):
    place = Place(*dims)
    core, partner = place.core, place.partner()
    half = left.shape[1]
    piece = both.shape[1]
    shard = piece // 2
    greet([partner] + place.neighbours())
    project(pair, left, total)

    def scatter(geometry):
        run_all(reduce_plane(total, inbox_a, inbox_b, piece, ssem=ring_send, rsem=ring_recv, **geometry))

    pl.when(core == 0)(lambda: scatter(row_first(place)))
    pl.when(core == 1)(lambda: scatter(column_first(place)))
    own = pl.ds(pl.multiple_of(place.chip() * piece, 8), piece)
    swap = remote(total.at[own, :], both.at[core], swap_send, swap_recv, partner)
    swap.start()
    both[core] = total[own, :]
    swap.wait_recv()
    value = exact_dot(both[0], w[:, :half], 1, 1) + exact_dot(both[1], w[:, half:], 1, 1)
    right[...] = jnp.where(core == 0, value[:shard], value[shard:])
    right_half[...] = jnp.where(core == 0, value[:, :half], value[:, half:]).astype(BF16)
    squares[...] = jnp.broadcast_to(jnp.sum(value * value, axis=0, keepdims=True), squares.shape)
    swap.wait_send()


def right_call(dims, pair, left, w):
    nz, ny, nx = dims
    columns = pair.shape[2]
    half = left.shape[1]
    rank = 2 * half
    chips = nz * ny
    piece = columns // chips
    ring = chips + max(nz, ny)
    dma = pltpu.SemaphoreType.DMA
    return pl.pallas_call(
        functools.partial(right_kernel, dims),
        out_shape=(
            jax.ShapeDtypeStruct((piece // 2, rank), F32),
            jax.ShapeDtypeStruct((piece, half), BF16),
            jax.ShapeDtypeStruct((8, rank), F32),
        ),
        in_specs=[VMEM_SPEC] * 3,
        out_specs=(VMEM_SPEC,) * 3,
        scratch_shapes=[
            pltpu.VMEM((columns, half), F32),
            pltpu.VMEM((chips, piece, half), F32),
            pltpu.VMEM((max(nz, ny), piece, half), F32),
            pltpu.VMEM((2, piece, half), F32),
            dma((ring,)), dma((ring,)), dma, dma,
        ],
        compiler_params=pltpu.CompilerParams(
            collective_id=2, has_side_effects=True, vmem_limit_bytes=VMEM_LIMIT
        ),
        name="right_factor",
    )(pair, left, w)


def share_kernel(dims, right_half, squares, gathered, norms, z_in, y_in, x_in,
                 ring_send, ring_recv, swap_send, swap_recv, send, recv):
    place = Place(*dims)
    nz, ny, nx = dims
    core, partner = place.core, place.partner()
    piece = right_half.shape[0]
    greet([partner] + place.x_peers() + place.y_peers() + place.z_peers())
    buf = gathered.at[core]
    at = lambda slot: pl.ds(pl.multiple_of(slot * piece, 16), piece)
    buf[at(place.chip()), :] = right_half[...]

    def level(inbox, me, peers, count, base, value):
        inbox[me] = value
        for o, peer in enumerate(peers, 1):
            remote(inbox.at[me], inbox.at[me], send.at[base + o], recv.at[base + o], peer).start()

    def level_done(inbox, me, peers, count, base):
        for o, peer in enumerate(peers, 1):
            there = inbox.at[wrap(me - o, count)]
            remote(there, there, send.at[base + o], recv.at[base + o], peer).wait_recv()
        total = inbox[0]
        for i in range(1, count):
            total = total + inbox[i]
        return total

    def drain(inbox, me, peers, base):
        for o, peer in enumerate(peers, 1):
            remote(inbox.at[me], inbox.at[me], send.at[base + o], recv.at[base + o], peer).wait_send()

    z_level = (z_in, place.z, place.z_peers(), nz, 0)
    y_level = (y_in, place.y, place.y_peers(), ny, nz)
    x_level = (x_in, place.x, place.x_peers(), nx, nz + ny)

    level(*z_level, squares[...])

    def after_z():
        level(*y_level, level_done(*z_level))

    def after_y():
        level(*x_level, level_done(*y_level))

    def after_x():
        norms[...] = level_done(*x_level)

    def forward(slot):
        here = buf.at[at(slot), :]
        remote(here, here, swap_send.at[slot], swap_recv.at[slot], partner).start()

    def run(geometry):
        gather_plane(buf, piece, ssem=ring_send, rsem=ring_recv, done=forward,
                     extras=(after_z, after_y, after_x), **geometry)

    pl.when(core == 0)(lambda: run(column_first(place)))
    pl.when(core == 1)(lambda: run(row_first(place)))

    for slot in range(nz * ny):
        there = gathered.at[1 - core, slot * piece : (slot + 1) * piece, :]
        remote(there, there, swap_send.at[slot], swap_recv.at[slot], partner).wait_recv()
    for slot in range(nz * ny):
        here = gathered.at[core, slot * piece : (slot + 1) * piece, :]
        remote(here, here, swap_send.at[slot], swap_recv.at[slot], partner).wait_send()
    for inbox, me, peers, count, base in (z_level, y_level, x_level):
        drain(inbox, me, peers, base)


def share_call(dims, right_half, squares):
    nz, ny, nx = dims
    piece, half = right_half.shape
    chips = nz * ny
    ring = chips + max(nz, ny)
    rank = 2 * half
    dma = pltpu.SemaphoreType.DMA
    return pl.pallas_call(
        functools.partial(share_kernel, dims),
        out_shape=(
            jax.ShapeDtypeStruct((2, chips * piece, half), BF16),
            jax.ShapeDtypeStruct((8, rank), F32),
        ),
        in_specs=[VMEM_SPEC] * 2,
        out_specs=(VMEM_SPEC,) * 2,
        scratch_shapes=[
            pltpu.VMEM((nz, 8, rank), F32),
            pltpu.VMEM((ny, 8, rank), F32),
            pltpu.VMEM((nx, 8, rank), F32),
            dma((ring,)), dma((ring,)), dma((chips,)), dma((chips,)),
            dma((nz + ny + nx,)), dma((nz + ny + nx,)),
        ],
        compiler_params=pltpu.CompilerParams(
            collective_id=3, has_side_effects=True, vmem_limit_bytes=VMEM_LIMIT
        ),
        name="share_right",
    )(right_half, squares)


def apply_kernel(step, momentum, gradient, ortho_half, update_left, gathered, momentum_next, update):
    half = gathered.shape[2]
    dims = (((1,), (1,)), ((), ()))

    def product(left):
        return sum(
            lax.dot_general(left[:, c * half : (c + 1) * half], gathered[c], dims, preferred_element_type=F32)
            for c in range(2)
        )

    blended = momentum[...] + gradient[...].astype(F32)
    momentum_next[...] = blended - step * product(ortho_half[...])
    update[...] = product(update_left[...]).astype(BF16)


def apply_call(step, momentum, gradient, ortho_half, update_left, gathered):
    rows, columns = momentum.shape
    rank = ortho_half.shape[1]
    width = 512 if columns % 512 == 0 else BLOCK
    tile = pl.BlockSpec((rows, width), lambda i: (0, i))
    whole = pl.BlockSpec((rows, rank), lambda i: (0, 0))
    return pl.pallas_call(
        functools.partial(apply_kernel, step),
        grid=(columns // width,),
        out_shape=(
            jax.ShapeDtypeStruct((rows, columns), F32),
            jax.ShapeDtypeStruct((rows, columns), BF16),
        ),
        in_specs=[tile, tile, whole, whole, pl.BlockSpec((2, width, rank // 2), lambda i: (0, i, 0))],
        out_specs=(tile, tile),
        compiler_params=pltpu.CompilerParams(vmem_limit_bytes=VMEM_LIMIT),
        name="apply",
    )(momentum, gradient, ortho_half, update_left, gathered)


def local(dims, momentum, gradient, right_prior):
    decay = 0.95
    prior = right_prior[0]
    blend_half = (momentum + gradient.astype(F32)).astype(BF16)
    left, pair = left_factor_call(dims, blend_half, prior)
    gram, left_rows = gram_call(dims, left)
    w, orthonormal = factor_call(gram, left_rows)
    right, right_half, squares = right_call(dims, pair, left, w)
    gathered, norms = share_call(dims, right_half, squares)
    column_scale = 1.0 / jnp.sqrt(norms[:1] + 1e-06)
    right_next = (right * column_scale).astype(BF16)[None]
    rows_all = momentum.shape[0] * lax.axis_size("fsdp")
    cols_all = momentum.shape[1] * lax.axis_size("tp")
    magnitude = math.sqrt(rows_all * cols_all / prior.shape[1])
    ortho_half = orthonormal.astype(BF16)
    update_left = (orthonormal * column_scale * magnitude).astype(BF16)
    momentum_next, update = apply_call(1.0 - decay, momentum, gradient, ortho_half, update_left, gathered)
    return (momentum_next, update, right_next)


def solution(mesh):
    fsdp, tp = mesh.shape["fsdp"], mesh.shape["tp"]
    dims = (fsdp // (2 * Y_CHIPS), Y_CHIPS, tp)
    in_specs = (P("fsdp", "tp"), P("fsdp", "tp"), P("tp", "fsdp", None))
    out_specs = (P("fsdp", "tp"), P("fsdp", "tp"), P("tp", "fsdp", None))
    return jax.shard_map(
        functools.partial(local, dims), mesh=mesh, in_specs=in_specs, out_specs=out_specs, check_vma=False
    )
```

time: 861 us -> 235 us (0.27); the launches traced: 850 us -> 234 us
  waiting for transfers between devices: 553 us -> 0 us
  Pallas kernels: 0 us -> 227 us
  other arithmetic: 144 us -> 7.01 us
  blocking collectives: 78.3 us -> 0 us
  matrix products: 36.7 us -> 0 us
  local copies, waits for them, and re-layouts: 20.6 us -> 0.01 us
  between operations: 17 us -> 0.67 us
    psum x2 -> x0, waiting for transfers between devices: 229 us -> none  [the longest x1 188 us: local(): lax.psum(jnp.dot(left_factor.T, left_factor, precision=lax.Precision.HIGH...]
    pallas_call x0 -> x6, Pallas kernels: none -> 227 us  [the longest x1 66.5 us: right_call(): pl.pallas_call(functools.partial(right_kernel, dims), out_shape=(jax.Shap...]
    all_gather x2 -> x0, waiting for transfers between devices: 166 us -> none  [the longest x1 88.5 us: local(): lax.all_gather(prior_block, 'fsdp', axis=0, tiled=True)]
    unnamed x6 -> x0, waiting for transfers between devices: 159 us -> none
    another operation x17 -> x0, other arithmetic: 136 us -> none  [the longest x14 92.7 us: local(): lower = jnp.linalg.cholesky(gram_matrix)]
    psum x1 -> x0, blocking collectives: 78.3 us -> none  [local(): totals = lax.psum(squares, ('fsdp', 'tp'))]
    dot_general x4 -> x0, matrix products: 21.2 us -> none  [the longest x1 6.87 us: local(): lax.dot_general(columns, ortho_half, (((0,), (0,)), ((), ())), preferred_...]
    another operation x17 -> x0, local copies, waits for them, and re-layouts: 15.7 us -> none
  transfers between devices with their start and end apart: 5 -> 0, of which waited for: 5 -> 0; matrix products, arithmetic and copies ran while one was open for 0% -> 0% of each run, Pallas kernels for 0% -> 0%
where the time goes in v1:
time: 235 us; the launch traced here: 234 us
  Pallas kernels  227 us (97%)
  other arithmetic  7.01 us (3%)
    pallas_call x1, Pallas kernels, right_call(): pl.pallas_call(functools.partial(right_kernel, dims), out_shape=(jax.Shap...  66.5 us
    pallas_call x1, Pallas kernels, left_factor_call(): pl.pallas_call(functools.partial(left_kernel, dims), out_shape=(jax.Shape...  52.2 us
    pallas_call x1, Pallas kernels, share_call(): pl.pallas_call(functools.partial(share_kernel, dims), out_shape=(jax.Shap...  40.2 us
    pallas_call x1, Pallas kernels, gram_call(): pl.pallas_call(functools.partial(gram_kernel, dims), out_shape=(jax.Shape...  32.5 us
    pallas_call x1, Pallas kernels, factor_call(): pl.pallas_call(factor_kernel, out_shape=(jax.ShapeDtypeStruct((rank, rank...  22.5 us
    pallas_call x1, Pallas kernels, apply_call(): pl.pallas_call(functools.partial(apply_kernel, step), grid=(columns // wi...  12.9 us

profile of v1, /device:TPU:1, one launch (start us, length us, event | category | flops | bytes accessed | tf_op | source)
XLA Modules:
  0.0 234.5 jit_solution(7609279196785989027)
XLA Ops:
  0.6 3.9 %add_convert_fusion.blend = bf16[128,6656]{1,0:T(8,128)(2,1)} fusion(f32[128,6656]{1,0:T(8,128)} %momentum.1, bf16[128,6656]{1,0:T(8,128)(2,1)} %gradient.1), kind=kLoop, calls=%fused_computation | loop fusion | flops 2555904 | bytes 6815744 | tf_op jit(solution)/shard_map/convert_element_type | solution.py:774
  4.6 52.2 %left_factor.1 = (f32[256,256]{1,0:T(8,128)}, bf16[2,128,6656]{2,1,0:T(8,128)(2,1)}) custom-call(bf16[128,6656]{1,0:T(8,128)(2,1)} %add_convert_fusion.blend, bf16[104,512]{1,0:T(8,128)(2,1)} %bitcast.4), custom_call_target="tpu_custom_call" | custom-call | tf_op jit(solution)/shard_map/left_factor/pallas_call | solution.py:404
  56.8 32.5 %gram.1 = (f32[512,512]{1,0:T(8,128)}, f32[128,512]{1,0:T(8,128)}) custom-call(f32[256,256]{1,0:T(8,128)} %get-tuple-element.16.left), custom_call_target="tpu_custom_call" | custom-call | tf_op jit(solution)/shard_map/gram/pallas_call | solution.py:517
  89.3 22.5 %factor.1 = (f32[512,512]{1,0:T(8,128)}, f32[128,512]{1,0:T(8,128)}) custom-call(f32[512,512]{1,0:T(8,128)} %get-tuple-element.17.gram, f32[128,512]{1,0:T(8,128)} %get-tuple-element.18.left), custom_call_target="tpu_custom_call" | custom-call | tf_op jit(solution)/shard_map/factor/pallas_call | solution.py:549
  111.8 0.0 copy-start
  111.8 66.5 %right_factor.1 = (f32[104,512]{1,0:T(8,128)}, bf16[208,256]{1,0:T(8,128)(2,1)}, f32[8,512]{1,0:T(8,128)}) custom-call(bf16[2,128,6656]{2,1,0:T(8,128)(2,1)} %get-tuple-element.20.pair, f32[256,256]{1,0:T(8,128)} %get-tuple-element.16.left, f32[512,512]{1,0:T(8,128)} %get-tuple-element.21.w), custom_call_target="tpu_custom_call" | custom-call | tf_op jit(solution)/shard_map/right_factor/pallas_call | solution.py:619
  178.3 40.2 %share_right.1 = (bf16[2,6656,256]{2,1,0:T(8,128)(2,1)}, f32[8,512]{1,0:T(8,128)}) custom-call(bf16[208,256]{1,0:T(8,128)(2,1)} %get-tuple-element.22.right_half, f32[8,512]{1,0:T(8,128)} %get-tuple-element.23.squares), custom_call_target="tpu_custom_call" | custom-call | tf_op jit(solution)/shard_map/share_right/pallas_call | solution.py:714
  218.5 0.7 add_rsqrt_fusion
  219.3 1.6 fusion
  220.9 0.0 copy-done
  220.9 0.7 multiply_convert_fusion
  221.6 12.9 %apply.1 = (f32[128,6656]{1,0:T(8,128)}, bf16[128,6656]{1,0:T(8,128)(2,1)}) custom-call(f32[128,6656]{1,0:T(8,128)} %momentum.1, bf16[128,6656]{1,0:T(8,128)(2,1)} %gradient.1, bf16[128,512]{1,0:T(8,128)(2,1)} %get-tuple-element.30.ortho_half, bf16[128,512]{1,0:T(8,128)(2,1)} %get-tuple-element.29.update_left, bf16[2,6656,256]{2,1,0:T(8,128)(2,1)} %get-tuple-element.25.gathered), custom_call_target="tpu_custom_call" | custom-call | tf_op jit(solution)/shard_map/apply/pallas_call | solution.py:757
Async XLA Ops:
  111.8 109.1 %copy-start = (f32[128,512]{1,0:T(8,128)S(1)}, f32[128,512]{1,0:T(8,128)}, u32[]{:S(2)}) copy-start(f32[128,512]{1,0:T(8,128)} %get-tuple-element.19) | copy-start | bytes 786436

commit v2 on v0

v2 whole, which is shorter than its diff:
```python
import functools
import math

import jax
import jax.numpy as jnp
from jax import lax
from jax.experimental import pallas as pl
from jax.experimental.pallas import tpu as pltpu
from jax.sharding import PartitionSpec as P

HIGHEST = lax.Precision.HIGHEST
MESH = pl.DeviceIdType.MESH
F32 = jnp.float32
BF16 = jnp.bfloat16
VMEM_SPEC = pl.BlockSpec(memory_space=pltpu.VMEM)
VMEM_LIMIT = 60 * 1024 * 1024
BLOCK = 128
Y_CHIPS = 4


def wrap(value, size):
    return lax.rem(value + size, size)


def exact_dot(a, b, a_dim, b_dim):
    return lax.dot_general(
        a, b, (((a_dim,), (b_dim,)), ((), ())), precision=HIGHEST, preferred_element_type=F32
    )


class Place:
    def __init__(self, nz, ny, nx):
        self.nz, self.ny, self.nx = nz, ny, nx
        index = lax.axis_index("fsdp")
        self.x = lax.axis_index("tp")
        self.core = lax.rem(index, 2)
        self.y = lax.rem(lax.div(index, 2), ny)
        self.z = lax.div(index, 2 * ny)

    def device(self, z=None, y=None, core=None, x=None):
        z = self.z if z is None else z
        y = self.y if y is None else y
        core = self.core if core is None else core
        x = self.x if x is None else x
        return ((z * self.ny + y) * 2 + core, x)

    def partner(self):
        return self.device(core=1 - self.core)

    def x_peers(self):
        return [self.device(x=wrap(self.x + o, self.nx)) for o in range(1, self.nx)]

    def y_peers(self):
        return [self.device(y=wrap(self.y + o, self.ny)) for o in range(1, self.ny)]

    def z_peers(self):
        return [self.device(z=wrap(self.z + o, self.nz)) for o in range(1, self.nz)]

    def chip(self):
        return self.z * self.ny + self.y


def greet(devices):
    barrier = pltpu.get_barrier_semaphore()
    for device in devices:
        pl.semaphore_signal(barrier, inc=1, device_id=device, device_id_type=MESH)
    pl.semaphore_wait(barrier, len(devices))


def remote(src, dst, send_sem, recv_sem, device):
    return pltpu.make_async_remote_copy(
        src_ref=src, dst_ref=dst, send_sem=send_sem, recv_sem=recv_sem,
        device_id=device, device_id_type=MESH,
    )


def halves(rows, unit):
    first = -(-(rows // 2) // unit) * unit
    return ((0, first), (first, rows - first))


class Plan:
    def __init__(self, place, z_first, offset, rows, unit):
        self.offset, self.rows = offset, rows
        first = -(-(rows // 2) // unit) * unit
        self.spans = ((0, first), (first, rows - first))
        self.unit = unit
        if z_first:
            self.na, self.nb, self.me_a, self.me_b = place.nz, place.ny, place.z, place.y
            self.slot = lambda a, b: a * place.ny + b
            self.device = lambda a, b: place.device(z=a, y=b)
        else:
            self.na, self.nb, self.me_a, self.me_b = place.ny, place.nz, place.y, place.z
            self.slot = lambda a, b: b * place.ny + a
            self.device = lambda a, b: place.device(z=b, y=a)
        self.half_a, self.half_b = self.na // 2, self.nb // 2
        self.sems = self.na + self.na * self.nb

    def span(self, part):
        return (0, self.rows) if part is None else self.spans[part]

    def at(self, a, b, piece, part=None):
        offset, size = self.span(part)
        start = self.slot(a, b) * piece + self.offset + offset
        return pl.ds(pl.multiple_of(start, self.unit), size)


def gather_events(plan, buf, piece, ssem, rsem, base, done):
    na, nb, half_a, half_b = plan.na, plan.nb, plan.half_a, plan.half_b
    me_a, me_b = plan.me_a, plan.me_b

    def copy(key, sending):
        kind, d, step, ra = key
        sign = 1 - 2 * d
        if kind == 0:
            part = d if step == half_a else None
            back = (0 if step <= 2 else 2) if sending else step
            a, b = wrap(me_a - sign * back, na), me_b
            target = plan.device(wrap(me_a + sign * (step - back), na), me_b)
            index = base + d * half_a + step - 1
        else:
            part = d if step == half_b else None
            a, b = wrap(me_a + ra, na), wrap(me_b - sign * (step - 1 if sending else step), nb)
            target = plan.device(me_a, wrap(me_b + sign, nb))
            index = base + na + (d * half_b + step - 1) * na + ra
        ref = buf.at[plan.at(a, b, piece, part), :]
        return remote(ref, ref, ssem.at[index], rsem.at[index], target)

    started = []

    def start(key):
        copy(key, True).start()
        started.append(key)

    def spread(ra):
        for d in (0, 1):
            start((1, d, 1, ra))

    landed = {}

    def whole(what):
        landed[what] = landed.get(what, 0) + 1
        return landed[what] == 2

    def begin():
        for step in range(1, min(half_a, 2) + 1):
            for d in (0, 1):
                start((0, d, step, 0))
        spread(0)
        done(plan, me_a, me_b)

    def first_ring(d, step):
        sign = 1 - 2 * d
        copy((0, d, step, 0), False).wait_recv()
        if step == 2:
            for later in range(3, half_a + 1):
                start((0, d, later, 0))
        if step < half_a or whole("a"):
            ra = (-sign * step) % na
            spread(ra)
            done(plan, wrap(me_a + ra, na), me_b)

    def second_ring(d, step, ra):
        sign = 1 - 2 * d
        copy((1, d, step, ra), False).wait_recv()
        if step < half_b:
            start((1, d, step + 1, ra))
        if step < half_b or whole(ra):
            done(plan, wrap(me_a + ra, na), wrap(me_b - sign * step, nb))

    def end():
        for key in started:
            copy(key, True).wait_send()

    when = {0: 0.0, 1: 1.0, 2: 1.4, 3: 2.4, 4: 2.8}
    events = []
    for step in range(1, half_a + 1):
        for d in (0, 1):
            events.append((when[step], functools.partial(first_ring, d, step)))
    for step in range(1, half_b + 1):
        for ra in range(na):
            for d in (0, 1):
                events.append((when[min(ra, na - ra)] + 0.05 + step, functools.partial(second_ring, d, step, ra)))
    return begin, events, end


def gather_plane(buf, piece, plans, ssem, rsem, done, extras=()):
    base, events, begins, ends = 0, [], [], []
    for plan in plans:
        begin, some, end = gather_events(plan, buf, piece, ssem, rsem, base, done)
        base += plan.sems
        begins.append(begin)
        ends.append(end)
        events += some
    for begin in begins:
        begin()
    events += list(extras)
    for _, action in sorted(events, key=lambda e: e[0]):
        action()
    for end in ends:
        end()


def far_first(n):
    return sorted(range(n), key=lambda j: (-min(j, n - j), j))


def reduce_events(plan, total, inbox_a, inbox_b, piece, ssem, rsem, base, per_chunk, hop):
    order = far_first(plan.nb)

    def ring(n, me, chunks, source, inbox, device, base):
        half = n // 2

        def index(d, step, j):
            return base + (d * half + step - 1) * len(chunks) + chunks.index(j)

        def landing(d, step, j, part):
            offset, size = plan.span(part)
            slot = (d * half + step - 1) * len(chunks) + chunks.index(j)
            return inbox.at[slot, pl.ds(offset, size), :]

        def copy(d, step, j):
            sign = 1 - 2 * d
            part = d if step == 1 else None
            if step == 1:
                src = total.at[source(wrap(me - sign * half, n), j, part), :]
            else:
                src = landing(d, step - 1, j, part)
            i = index(d, step, j)
            return remote(src, landing(d, step, j, part), ssem.at[i], rsem.at[i], device(wrap(me - sign, n)))

        def send(j):
            for d in (0, 1):
                copy(d, 1, j).start()

        def receive(d, step, j):
            sign = 1 - 2 * d
            copy(d, step, j).wait_recv()
            if step < half:
                dest = wrap(me - sign * (half - step), n)
                for part in (0, 1):
                    here = landing(d, step, j, part)
                    own = total[source(dest, j, part), :]
                    here[...] = own if step == 1 and part != d else here[...] + own
                copy(d, step + 1, j).start()
            else:
                part = d if step == 1 else None
                own = source(me, j, part)
                total[own, :] = total[own, :] + landing(d, step, j, part)[...]

        def end():
            for step in range(1, half + 1):
                for j in chunks:
                    for d in (0, 1):
                        copy(d, step, j).wait_send()

        return send, receive, end

    na, nb = plan.na, plan.nb
    send_a, receive_a, end_a = ring(
        na, plan.me_a, order,
        lambda dest, j, part: plan.at(dest, wrap(plan.me_b + j, nb), piece, part),
        inbox_a, lambda a: plan.device(a, plan.me_b), base,
    )
    send_b, receive_b, end_b = ring(
        nb, plan.me_b, [0],
        lambda dest, j, part: plan.at(plan.me_a, dest, piece, part),
        inbox_b, lambda b: plan.device(plan.me_a, b), base + na * nb,
    )
    events = []
    ready = {}
    for pos, j in enumerate(order):
        events.append((max(0.0, per_chunk * (pos - 1)), functools.partial(send_a, j)))
        for step in range(1, plan.half_a + 1):
            at = per_chunk * pos + hop * step
            for d in (0, 1):
                events.append((at + 0.01 * d, functools.partial(receive_a, d, step, j)))
        ready[min(j, nb - j)] = per_chunk * pos + hop * plan.half_a + 0.1
    events.append((ready[plan.half_b], functools.partial(send_b, 0)))
    at = ready[plan.half_b]
    for step in range(1, plan.half_b + 1):
        at = max(at + hop, ready[plan.half_b - step] + 0.1)
        for d in (0, 1):
            events.append((at + 0.01 * d, functools.partial(receive_b, d, step, 0)))

    def end():
        end_a()
        end_b()

    return events, end


def rows_of(tile, k):
    return jnp.broadcast_to(tile[k : k + 1, :], tile.shape)


def columns_of(tile, k):
    return jnp.broadcast_to(tile[:, k : k + 1], tile.shape)


def inverse_factor(block):
    count = BLOCK // 8
    d = [block[8 * i : 8 * i + 8, :] for i in range(count)]
    row = lax.broadcasted_iota(jnp.int32, (8, BLOCK), 0)
    lane = lax.broadcasted_iota(jnp.int32, (8, BLOCK), 1)
    e = [(row + 8 * i == lane).astype(F32) for i in range(count)]
    out = []
    for s in range(count):
        c = [[columns_of(d[i], 8 * s + k) for k in range(8)] for i in range(s, count)]
        pivots = jnp.zeros((8, BLOCK), F32)
        for k in range(8):
            pivot = rows_of(c[0][k], k)
            inverse = 1.0 / pivot
            pivots = jnp.where(row == k, pivot, pivots)
            d_row, e_row = rows_of(d[s], k), rows_of(e[s], k)
            later = [rows_of(c[0][q], k) for q in range(k + 1, 8)]
            for i in range(s, count):
                factor = c[i - s][k] * inverse
                if i == s:
                    factor = jnp.where(row > k, factor, 0.0)
                d[i] = d[i] - factor * d_row
                e[i] = e[i] - factor * e_row
                for q in range(k + 1, 8):
                    c[i - s][q] = c[i - s][q] - factor * later[q - k - 1]
        out.append(e[s] * lax.rsqrt(pivots))
        if s % 2:
            yield 0.6
    return jnp.concatenate(out, axis=0)


def factor_steps(a, w):
    size = a.shape[0]
    w[...] = jnp.zeros((size, size), F32)
    for o in range(0, size, BLOCK):
        end = o + BLOCK
        inverse = yield from inverse_factor(a[o:end, o:end])
        w[o:end, o:end] = inverse
        if end < size:
            low = exact_dot(a[end:, o:end], inverse, 1, 1)
            a[end:, o:end] = low
            a[end:, end:] = a[end:, end:] - exact_dot(low, low, 1, 1)
        yield 0.5
        if o:
            through = exact_dot(a[o:end, :o], w[:o, :o], 1, 0)
            w[o:end, :o] = -exact_dot(inverse, through, 1, 0)
        yield 0.3


class Mail:
    def __init__(self, send, recv):
        self.send, self.recv, self.used, self.sent = send, recv, 0, []

    def take(self, count):
        self.used += count
        return self.used - count

    def start(self, src, dst, index, device):
        copy = remote(src, dst, self.send.at[index], self.recv.at[index], device)
        copy.start()
        self.sent.append(copy)

    def wait(self, ref, index, device):
        remote(ref, ref, self.send.at[index], self.recv.at[index], device).wait_recv()

    def end(self):
        for copy in self.sent:
            copy.wait_send()


def left_sum(place, mail, partial, inbox, left):
    nx = place.nx
    part = partial.shape[0] // nx
    peers = place.x_peers()
    at = lambda x: pl.ds(pl.multiple_of(x * part, 8), part)
    base = mail.take(nx)
    for o, peer in enumerate(peers, 1):
        mail.start(partial.at[at(wrap(place.x + o, nx)), :], inbox.at[o], base + o, peer)
    total = partial[at(place.x), :]
    for o, peer in enumerate(peers, 1):
        mail.wait(inbox.at[o], base + o, peer)
        total = total + inbox[o]
    left[at(place.x), :] = total
    base = mail.take(nx)
    for o, peer in enumerate(peers, 1):
        mail.start(left.at[at(place.x), :], left.at[at(place.x), :], base + o, peer)
    for o, peer in enumerate(peers, 1):
        mail.wait(left.at[at(wrap(place.x - o, nx)), :], base + o, peer)


def gram_steps(place, mail, left, both, part, z_in, y_in, gram, meanwhile):
    core, partner = place.core, place.partner()
    nz, ny, nx = place.nz, place.ny, place.nx
    half = left.shape[1]
    across = 2 * half // nx
    rows = across // nz

    i = mail.take(1)
    mail.start(left, both.at[core], i, partner)
    both[core] = left[...]
    mail.wait(both.at[1 - core], i, partner)
    per = half // across
    lanes = pl.ds(pl.multiple_of(lax.rem(place.x, per) * across, BLOCK), across)
    part[...] = exact_dot(both[lax.div(place.x, per), :, lanes], left[...], 0, 0)

    z_peers, y_peers, x_peers = place.z_peers(), place.y_peers(), place.x_peers()
    at_z = lambda z: pl.ds(pl.multiple_of(z * rows, 8), rows)
    i = mail.take(nz)
    for o, peer in enumerate(z_peers, 1):
        mail.start(part.at[at_z(wrap(place.z + o, nz)), :], z_in.at[o], i + o, peer)
    meanwhile()
    yield 0.0
    total = part[at_z(place.z), :]
    for o, peer in enumerate(z_peers, 1):
        mail.wait(z_in.at[o], i + o, peer)
        total = total + z_in[o]
    i = mail.take(ny)
    y_in[place.y] = total
    for o, peer in enumerate(y_peers, 1):
        mail.start(y_in.at[place.y], y_in.at[place.y], i + o, peer)
    yield 3.5
    for o, peer in enumerate(y_peers, 1):
        mail.wait(y_in.at[wrap(place.y - o, ny)], i + o, peer)
    total = y_in[0]
    for y in range(1, ny):
        total = total + y_in[y]

    def at(x, z):
        return gram.at[core, pl.ds(pl.multiple_of(x * across + z * rows, 8), rows), :]

    at(place.x, place.z)[...] = total
    i = mail.take(nz)
    for o, peer in enumerate(z_peers, 1):
        mail.start(at(place.x, place.z), at(place.x, place.z), i + o, peer)
    yield 5.0
    for o, peer in enumerate(z_peers, 1):
        mail.wait(at(place.x, wrap(place.z - o, nz)), i + o, peer)
    whole = lambda x: gram.at[core, pl.ds(pl.multiple_of(x * across, 8), across), :]
    i = mail.take(nx)
    for o, peer in enumerate(x_peers, 1):
        mail.start(whole(place.x), whole(place.x), i + o, peer)
    yield 5.5
    for o, peer in enumerate(x_peers, 1):
        mail.wait(whole(wrap(place.x - o, nx)), i + o, peer)
    i = mail.take(1)
    mail.start(gram.at[core], gram.at[core], i, partner)
    yield 1.5
    mail.wait(gram.at[1 - core], i, partner)


def project(pair, left, total):
    rows, columns = pair.shape[1:]
    half = left.shape[1]
    upper = left[...].astype(BF16)
    lower = (left[...] - upper.astype(F32)).astype(BF16)
    both = jnp.concatenate([upper, lower], axis=1)
    width = 512 if columns % 512 == 0 else BLOCK

    @pl.loop(0, columns // width)
    def _(i):
        at = pl.ds(pl.multiple_of(i * width, BLOCK), width)
        value = sum(
            lax.dot_general(pair[c, :, at], both[c * rows : (c + 1) * rows], (((0,), (0,)), ((), ())),
                            preferred_element_type=F32)
            for c in range(2)
        )
        total[at, :] = value[:, :half] + value[:, half:]


def merge(steps, events, begin=0.0):
    events = sorted(events, key=lambda e: e[0])
    now = begin
    for spent in steps:
        now += spent
        while events and events[0][0] <= now:
            events.pop(0)[1]()
    for _, action in events:
        action()


def step_kernel(dims, magnitude, momentum, gradient, prior, gathered, stacked, right_next,
                mom, grad, pair, mine, given, buf, partial, x_in, left, both, part, z_in, y_in, gram,
                a, w, total, in_yz, in_z, in_zy, in_y, pieces, ortho, nz_in, ny_in, nx_in,
                load_sem, one_send, one_recv, two_send, two_recv, sum_send, sum_recv,
                swap_send, swap_recv, send, recv):
    place = Place(*dims)
    nz, ny, nx = dims
    core, partner = place.core, place.partner()
    shard, rank = prior.shape
    half = rank // 2
    rows, columns = mom.shape
    piece = 2 * shard
    long = 128 if piece == 208 else 32
    loads = [pltpu.make_async_copy(momentum, mom, load_sem.at[0]), pltpu.make_async_copy(gradient, grad, load_sem.at[1])]
    for load in loads:
        load.start()
    greet([partner] + place.x_peers() + place.y_peers() + place.z_peers())
    mail = Mail(send, recv)

    low, high = prior[:, :half].astype(F32), prior[:, half:].astype(F32)
    given[...] = jnp.where(core == 0, high, low)
    at_mine = mine.at[pl.ds(pl.multiple_of(core * shard, 8), shard), :]
    at_theirs = mine.at[pl.ds(pl.multiple_of((1 - core) * shard, 8), shard), :]
    i = mail.take(1)
    mail.start(given, at_mine, i, partner)
    at_mine[...] = jnp.where(core == 0, low, high)
    mail.wait(at_theirs, i, partner)
    at_chip = lambda slot: pl.ds(pl.multiple_of(slot * piece, 16), piece)
    buf[at_chip(place.chip()), :] = mine[...].astype(BF16)
    swap_blend = mail.take(1)

    def blend():
        for load in loads:
            load.wait()
        width = 512 if columns % 512 == 0 else BLOCK

        @pl.loop(0, columns // width)
        def _(i):
            at = pl.ds(pl.multiple_of(i * width, BLOCK), width)
            pair[core, :, at] = (mom[:, at] + grad[:, at].astype(F32)).astype(BF16)

        mail.start(pair.at[core], pair.at[core], swap_blend, partner)

    plans = lambda unit: (Plan(place, True, 0, long, unit), Plan(place, False, long, piece - long, unit))
    gather_plane(buf, piece, plans(16), one_send, one_recv, lambda *_: None, [(0.5, blend)])
    mail.wait(pair.at[1 - core], swap_blend, partner)

    width = 1664 if columns % 1664 == 0 else BLOCK
    partial[...] = jnp.zeros_like(partial)

    @pl.loop(0, columns // width)
    def _(i):
        at = pl.ds(pl.multiple_of(i * width, BLOCK), width)
        for c in range(2):
            own = slice(c * rows, (c + 1) * rows)
            partial[own, :] += jnp.dot(pair[c, :, at], buf[at, :], preferred_element_type=F32)

    left_sum(place, mail, partial, x_in, left)

    bulk_y = Plan(place, False, 0, long, 8)
    bulk_z = Plan(place, True, long, piece - long, 8)
    events_y, end_y = reduce_events(bulk_y, total, in_yz, in_z, piece, sum_send, sum_recv, 0, 4.5, 4.5)
    events_z, end_z = reduce_events(bulk_z, total, in_zy, in_y, piece, sum_send, sum_recv, nz * ny + nz, 6.6, 4.0)

    def chain():
        yield from gram_steps(place, mail, left, both, part, z_in, y_in, gram, lambda: project(pair, left, total))
        for c in range(2):
            a[:, c * half : (c + 1) * half] = gram[c]
        yield from factor_steps(a, w)
        own = pl.ds(pl.multiple_of(core * rows, 8), rows)
        ortho[...] = exact_dot(both[0, own, :], w[:, :half], 1, 1) + exact_dot(both[1, own, :], w[:, half:], 1, 1)
        yield 1.0

    merge(chain(), events_y + events_z)

    own = pl.ds(pl.multiple_of(place.chip() * piece, 8), piece)
    i = mail.take(1)
    mail.start(total.at[own, :], pieces.at[core], i, partner)
    pieces[core] = total[own, :]
    mail.wait(pieces.at[1 - core], i, partner)
    value = exact_dot(pieces[0], w[:, :half], 1, 1) + exact_dot(pieces[1], w[:, half:], 1, 1)
    squares = jnp.broadcast_to(jnp.sum(value * value, axis=0, keepdims=True), (8, rank))
    right = jnp.where(core == 0, value[:shard], value[shard:])
    share = gathered.at[core]
    share[at_chip(place.chip()), :] = jnp.where(core == 0, value[:, :half], value[:, half:]).astype(BF16)

    def level(inbox, me, peers, count):
        return inbox, me, peers, count, mail.take(count)

    def level_start(inbox, me, peers, count, base, value):
        inbox[me] = value
        for o, peer in enumerate(peers, 1):
            mail.start(inbox.at[me], inbox.at[me], base + o, peer)

    def level_done(inbox, me, peers, count, base):
        for o, peer in enumerate(peers, 1):
            mail.wait(inbox.at[wrap(me - o, count)], base + o, peer)
        total = inbox[0]
        for i in range(1, count):
            total = total + inbox[i]
        return total

    z_level = level(nz_in, place.z, place.z_peers(), nz)
    y_level = level(ny_in, place.y, place.y_peers(), ny)
    x_level = level(nx_in, place.x, place.x_peers(), nx)
    level_start(*z_level, squares)

    def finish():
        column_scale = 1.0 / jnp.sqrt(level_done(*x_level)[:1] + 1e-06)
        right_next[...] = (right * column_scale).astype(BF16)
        stacked[:rows, :] = ortho[...].astype(BF16)
        stacked[rows:, :] = (ortho[...] * column_scale * magnitude).astype(BF16)

    def forward(plan, a, b):
        offset = 0 if plan.offset == 0 else nz * ny
        here = share.at[plan.at(a, b, piece), :]
        slot = offset + plan.slot(a, b)
        remote(here, here, swap_send.at[slot], swap_recv.at[slot], partner).start()

    gather_plane(share, piece, plans(16), two_send, two_recv, forward, [
        (1.2, lambda: level_start(*y_level, level_done(*z_level))),
        (2.0, lambda: level_start(*x_level, level_done(*y_level))),
        (3.0, finish),
    ])
    for offset, size, base in ((0, long, 0), (long, piece - long, nz * ny)):
        for slot in range(nz * ny):
            at = slice(slot * piece + offset, slot * piece + offset + size)
            there, here = gathered.at[1 - core, at, :], gathered.at[core, at, :]
            remote(there, there, swap_send.at[base + slot], swap_recv.at[base + slot], partner).wait_recv()
            remote(here, here, swap_send.at[base + slot], swap_recv.at[base + slot], partner).wait_send()
    end_y()
    end_z()
    mail.end()


def step_call(dims, magnitude, momentum, gradient, prior):
    nz, ny, nx = dims
    shard, rank = prior.shape
    rows, columns = momentum.shape
    half = rank // 2
    piece = 2 * shard
    long = 128 if piece == 208 else 32
    chips = nz * ny
    across = rank // nx
    ring = 2 * chips + nz + ny
    mails = 5 + 4 * nx + 3 * nz + 2 * ny
    dma = pltpu.SemaphoreType.DMA
    vmem = pltpu.VMEM
    return pl.pallas_call(
        functools.partial(step_kernel, dims, magnitude),
        out_shape=(
            jax.ShapeDtypeStruct((2, columns, half), BF16),
            jax.ShapeDtypeStruct((2 * rows, rank), BF16),
            jax.ShapeDtypeStruct((shard, rank), BF16),
        ),
        in_specs=[pl.BlockSpec(memory_space=pl.ANY)] * 2 + [VMEM_SPEC],
        out_specs=(VMEM_SPEC,) * 3,
        scratch_shapes=[
            vmem((rows, columns), F32), vmem((rows, columns), BF16),
            vmem((2, rows, columns), BF16),
            vmem((piece, half), F32), vmem((shard, half), F32), vmem((columns, half), BF16),
            vmem((2 * rows, half), F32), vmem((nx, 2 * rows // nx, half), F32), vmem((2 * rows, half), F32),
            vmem((2, 2 * rows, half), F32), vmem((across, half), F32),
            vmem((nz, across // nz, half), F32), vmem((ny, across // nz, half), F32),
            vmem((2, rank, half), F32), vmem((rank, rank), F32), vmem((rank, rank), F32),
            vmem((columns, half), F32),
            vmem((chips, long, half), F32), vmem((nz, long, half), F32),
            vmem((chips, piece - long, half), F32), vmem((ny, piece - long, half), F32),
            vmem((2, piece, half), F32), vmem((rows, rank), F32),
            vmem((nz, 8, rank), F32), vmem((ny, 8, rank), F32), vmem((nx, 8, rank), F32),
            dma((2,)), dma((ring,)), dma((ring,)), dma((ring,)), dma((ring,)), dma((ring,)), dma((ring,)),
            dma((2 * chips,)), dma((2 * chips,)), dma((mails,)), dma((mails,)),
        ],
        compiler_params=pltpu.CompilerParams(
            collective_id=0, has_side_effects=True, vmem_limit_bytes=VMEM_LIMIT
        ),
        name="dion_step",
    )(momentum, gradient, prior)


def apply_kernel(step, momentum, gradient, stacked, gathered, momentum_next, update):
    half = gathered.shape[2]
    rows = momentum.shape[0]
    dims = (((1,), (1,)), ((), ()))
    products = sum(
        lax.dot_general(stacked[:, c * half : (c + 1) * half], gathered[c], dims, preferred_element_type=F32)
        for c in range(2)
    )
    blended = momentum[...] + gradient[...].astype(F32)
    momentum_next[...] = blended - step * products[:rows]
    update[...] = products[rows:].astype(BF16)


def apply_call(step, momentum, gradient, stacked, gathered):
    rows, columns = momentum.shape
    rank = stacked.shape[1]
    width = 512 if columns % 512 == 0 else BLOCK
    tile = pl.BlockSpec((rows, width), lambda i: (0, i))
    return pl.pallas_call(
        functools.partial(apply_kernel, step),
        grid=(columns // width,),
        out_shape=(
            jax.ShapeDtypeStruct((rows, columns), F32),
            jax.ShapeDtypeStruct((rows, columns), BF16),
        ),
        in_specs=[
            tile, tile, pl.BlockSpec(stacked.shape, lambda i: (0, 0)),
            pl.BlockSpec((2, width, rank // 2), lambda i: (0, i, 0)),
        ],
        out_specs=(tile, tile),
        compiler_params=pltpu.CompilerParams(vmem_limit_bytes=VMEM_LIMIT),
        name="apply",
    )(momentum, gradient, stacked, gathered)


def local(dims, momentum, gradient, right_prior):
    decay = 0.95
    prior = right_prior[0]
    rows_all = momentum.shape[0] * lax.axis_size("fsdp")
    cols_all = momentum.shape[1] * lax.axis_size("tp")
    magnitude = math.sqrt(rows_all * cols_all / prior.shape[1])
    gathered, stacked, right_next = step_call(dims, magnitude, momentum, gradient, prior)
    momentum_next, update = apply_call(1.0 - decay, momentum, gradient, stacked, gathered)
    return (momentum_next, update, right_next[None])


def solution(mesh):
    fsdp, tp = mesh.shape["fsdp"], mesh.shape["tp"]
    dims = (fsdp // (2 * Y_CHIPS), Y_CHIPS, tp)
    in_specs = (P("fsdp", "tp"), P("fsdp", "tp"), P("tp", "fsdp", None))
    out_specs = (P("fsdp", "tp"), P("fsdp", "tp"), P("tp", "fsdp", None))
    return jax.shard_map(
        functools.partial(local, dims), mesh=mesh, in_specs=in_specs, out_specs=out_specs, check_vma=False
    )
```

time: 861 us -> 173 us (0.20); the launches traced: 850 us -> 173 us
  waiting for transfers between devices: 553 us -> 0 us
  Pallas kernels: 0 us -> 172 us
  other arithmetic: 144 us -> 0 us
  blocking collectives: 78.3 us -> 0 us
  matrix products: 36.7 us -> 0 us
  local copies, waits for them, and re-layouts: 20.6 us -> 0.65 us
  between operations: 17 us -> 0.65 us
    psum x2 -> x0, waiting for transfers between devices: 229 us -> none  [the longest x1 188 us: local(): lax.psum(jnp.dot(left_factor.T, left_factor, precision=lax.Precision.HIGH...]
    pallas_call x0 -> x2, Pallas kernels: none -> 172 us  [the longest x1 159 us: step_call(): pl.pallas_call(functools.partial(step_kernel, dims, magnitude), out_shape...]
    all_gather x2 -> x0, waiting for transfers between devices: 166 us -> none  [the longest x1 88.5 us: local(): lax.all_gather(prior_block, 'fsdp', axis=0, tiled=True)]
    unnamed x6 -> x0, waiting for transfers between devices: 159 us -> none
    another operation x17 -> x0, other arithmetic: 136 us -> none  [the longest x14 92.7 us: local(): lower = jnp.linalg.cholesky(gram_matrix)]
    psum x1 -> x0, blocking collectives: 78.3 us -> none  [local(): totals = lax.psum(squares, ('fsdp', 'tp'))]
    dot_general x4 -> x0, matrix products: 21.2 us -> none  [the longest x1 6.87 us: local(): lax.dot_general(columns, ortho_half, (((0,), (0,)), ((), ())), preferred_...]
    another operation x17 -> x0, local copies, waits for them, and re-layouts: 15.7 us -> none
  transfers between devices with their start and end apart: 5 -> 0, of which waited for: 5 -> 0; matrix products, arithmetic and copies ran while one was open for 0% -> 0% of each run, Pallas kernels for 0% -> 0%
where the time goes in v2:
time: 173 us
  Pallas kernels  172 us (99%)
    pallas_call x1, Pallas kernels, step_call(): pl.pallas_call(functools.partial(step_kernel, dims, magnitude), out_shape...  159 us
    pallas_call x1, Pallas kernels, apply_call(): pl.pallas_call(functools.partial(apply_kernel, step), grid=(columns // wi...  12.5 us

profile of v2, /device:TPU:1, one launch (start us, length us, event | category | flops | bytes accessed | tf_op | source)
XLA Modules:
  0.0 173.0 jit_solution(7787224567607148825)
XLA Ops:
  0.6 159.2 %dion_step.1 = (bf16[2,6656,256]{2,1,0:T(8,128)(2,1)}, bf16[256,512]{1,0:T(8,128)(2,1)}, bf16[104,512]{1,0:T(8,128)(2,1)}) custom-call(f32[128,6656]{1,0:T(8,128)} %momentum.3, bf16[128,6656]{1,0:T(8,128)(2,1)} %gradient.3, bf16[104,512]{1,0:T(8,128)(2,1)} %bitcast.3), custom_call_target="tpu_custom_call" | custom-call | tf_op jit(solution)/shard_map/dion_step/pallas_call | solution.py:628
  159.8 0.0 copy-start
  159.9 12.5 %apply.1 = (f32[128,6656]{1,0:T(8,128)}, bf16[128,6656]{1,0:T(8,128)(2,1)}) custom-call(f32[128,6656]{1,0:T(8,128)} %momentum.3, bf16[128,6656]{1,0:T(8,128)(2,1)} %gradient.3, bf16[256,512]{1,0:T(8,128)(2,1)} %get-tuple-element.8.stacked, bf16[2,6656,256]{2,1,0:T(8,128)(2,1)} %get-tuple-element.9.gathered), custom_call_target="tpu_custom_call" | custom-call | tf_op jit(solution)/shard_map/apply/pallas_call | solution.py:678
  172.4 0.0 copy-done
  172.4 0.6 copy.7
Async XLA Ops:
  159.8 12.5 %copy-start = (bf16[104,512]{1,0:T(8,128)(2,1)S(1)}, bf16[104,512]{1,0:T(8,128)(2,1)}, u32[]{:S(2)}) copy-start(bf16[104,512]{1,0:T(8,128)(2,1)} %get-tuple-element.12) | copy-start | bytes 319492

commit v3 on v2

--- a/solution.py
+++ b/solution.py
@@ -7,6 +7,13 @@
 from jax.experimental import pallas as pl
 from jax.experimental.pallas import tpu as pltpu
 from jax.sharding import PartitionSpec as P
+
+PER_Y, HOP_Y, PER_Z, HOP_Z = 4.5, 4.5, 9.0, 4.0
+GRAM_TIMES = (0.0, 3.5, 5.0, 5.5, 1.5)
+FACTOR_SCALE = 1.0
+SUM_LONG = 128
+WHEN = {0: 0.0, 1: 1.0, 2: 1.4, 3: 2.4, 4: 2.8}
+PACE_Y, PACE_Z = 1.0, 1.0
 
 HIGHEST = lax.Precision.HIGHEST
 MESH = pl.DeviceIdType.MESH
@@ -172,7 +179,7 @@
         for key in started:
             copy(key, True).wait_send()
 
-    when = {0: 0.0, 1: 1.0, 2: 1.4, 3: 2.4, 4: 2.8}
+    when, pace = WHEN, PACE_Y if plan.half_b == 2 else PACE_Z
     events = []
     for step in range(1, half_a + 1):
         for d in (0, 1):
@@ -180,7 +187,7 @@
     for step in range(1, half_b + 1):
         for ra in range(na):
             for d in (0, 1):
-                events.append((when[min(ra, na - ra)] + 0.05 + step, functools.partial(second_ring, d, step, ra)))
+                events.append((when[min(ra, na - ra)] + 0.05 + pace * step, functools.partial(second_ring, d, step, ra)))
     return begin, events, end
 
 
@@ -270,7 +277,7 @@
     events = []
     ready = {}
     for pos, j in enumerate(order):
-        events.append((max(0.0, per_chunk * (pos - 1)), functools.partial(send_a, j)))
+        events.append((0.0 if pos == 0 else max(0.1, per_chunk * (pos - 1)), functools.partial(send_a, j)))
         for step in range(1, plan.half_a + 1):
             at = per_chunk * pos + hop * step
             for d in (0, 1):
@@ -324,7 +331,7 @@
                     c[i - s][q] = c[i - s][q] - factor * later[q - k - 1]
         out.append(e[s] * lax.rsqrt(pivots))
         if s % 2:
-            yield 0.6
+            yield 0.072 * (17 - s) * FACTOR_SCALE
     return jnp.concatenate(out, axis=0)
 
 
@@ -339,11 +346,11 @@
             low = exact_dot(a[end:, o:end], inverse, 1, 1)
             a[end:, o:end] = low
             a[end:, end:] = a[end:, end:] - exact_dot(low, low, 1, 1)
-        yield 0.5
+        yield 0.5 * FACTOR_SCALE
         if o:
             through = exact_dot(a[o:end, :o], w[:o, :o], 1, 0)
             w[o:end, :o] = -exact_dot(inverse, through, 1, 0)
-        yield 0.3
+        yield 0.3 * FACTOR_SCALE
 
 
 class Mail:
@@ -408,7 +415,7 @@
     for o, peer in enumerate(z_peers, 1):
         mail.start(part.at[at_z(wrap(place.z + o, nz)), :], z_in.at[o], i + o, peer)
     meanwhile()
-    yield 0.0
+    yield GRAM_TIMES[0]
     total = part[at_z(place.z), :]
     for o, peer in enumerate(z_peers, 1):
         mail.wait(z_in.at[o], i + o, peer)
@@ -417,7 +424,7 @@
     y_in[place.y] = total
     for o, peer in enumerate(y_peers, 1):
         mail.start(y_in.at[place.y], y_in.at[place.y], i + o, peer)
-    yield 3.5
+    yield GRAM_TIMES[1]
     for o, peer in enumerate(y_peers, 1):
         mail.wait(y_in.at[wrap(place.y - o, ny)], i + o, peer)
     total = y_in[0]
@@ -431,35 +438,38 @@
     i = mail.take(nz)
     for o, peer in enumerate(z_peers, 1):
         mail.start(at(place.x, place.z), at(place.x, place.z), i + o, peer)
-    yield 5.0
+    yield GRAM_TIMES[2]
     for o, peer in enumerate(z_peers, 1):
         mail.wait(at(place.x, wrap(place.z - o, nz)), i + o, peer)
     whole = lambda x: gram.at[core, pl.ds(pl.multiple_of(x * across, 8), across), :]
     i = mail.take(nx)
     for o, peer in enumerate(x_peers, 1):
         mail.start(whole(place.x), whole(place.x), i + o, peer)
-    yield 5.5
+    yield GRAM_TIMES[3]
     for o, peer in enumerate(x_peers, 1):
         mail.wait(whole(wrap(place.x - o, nx)), i + o, peer)
     i = mail.take(1)
     mail.start(gram.at[core], gram.at[core], i, partner)
-    yield 1.5
+    yield GRAM_TIMES[4]
     mail.wait(gram.at[1 - core], i, partner)
 
 
-def project(pair, left, total):
-    rows, columns = pair.shape[1:]
-    half = left.shape[1]
+def split_terms(left):
     upper = left[...].astype(BF16)
     lower = (left[...] - upper.astype(F32)).astype(BF16)
-    both = jnp.concatenate([upper, lower], axis=1)
-    width = 512 if columns % 512 == 0 else BLOCK
-
-    @pl.loop(0, columns // width)
+    return jnp.concatenate([upper, lower], axis=1)
+
+
+def project(pair, terms, total, begin, size):
+    rows = pair.shape[1]
+    half = total.shape[1]
+    width = next(w for w in (832, 512, 384, BLOCK) if size % w == 0 and w % BLOCK == 0)
+
+    @pl.loop(0, size // width)
     def _(i):
-        at = pl.ds(pl.multiple_of(i * width, BLOCK), width)
+        at = pl.ds(pl.multiple_of(begin + i * width, BLOCK), width)
         value = sum(
-            lax.dot_general(pair[c, :, at], both[c * rows : (c + 1) * rows], (((0,), (0,)), ((), ())),
+            lax.dot_general(pair[c, :, at], terms[c * rows : (c + 1) * rows, :], (((0,), (0,)), ((), ())),
                             preferred_element_type=F32)
             for c in range(2)
         )
@@ -479,7 +489,7 @@
 
 def step_kernel(dims, magnitude, momentum, gradient, prior, gathered, stacked, right_next,
                 mom, grad, pair, mine, given, buf, partial, x_in, left, both, part, z_in, y_in, gram,
-                a, w, total, in_yz, in_z, in_zy, in_y, pieces, ortho, nz_in, ny_in, nx_in,
+                a, w, total, terms, in_yz, in_z, in_zy, in_y, pieces, ortho, nz_in, ny_in, nx_in,
                 load_sem, one_send, one_recv, two_send, two_recv, sum_send, sum_recv,
                 swap_send, swap_recv, send, recv):
     place = Place(*dims)
@@ -536,13 +546,26 @@
 
     left_sum(place, mail, partial, x_in, left)
 
-    bulk_y = Plan(place, False, 0, long, 8)
-    bulk_z = Plan(place, True, long, piece - long, 8)
-    events_y, end_y = reduce_events(bulk_y, total, in_yz, in_z, piece, sum_send, sum_recv, 0, 4.5, 4.5)
-    events_z, end_z = reduce_events(bulk_z, total, in_zy, in_y, piece, sum_send, sum_recv, nz * ny + nz, 6.6, 4.0)
+    sum_long = SUM_LONG if piece == 208 else 32
+    bulk_y = Plan(place, False, 0, sum_long, 8)
+    bulk_z = Plan(place, True, sum_long, piece - sum_long, 8)
+    events_y, end_y = reduce_events(bulk_y, total, in_yz, in_z, piece, sum_send, sum_recv, 0, PER_Y, HOP_Y)
+    events_z, end_z = reduce_events(bulk_z, total, in_zy, in_y, piece, sum_send, sum_recv, nz * ny + nz, PER_Z, HOP_Z)
+
+    terms[...] = split_terms(left)
+    parts = nz // 2
+    size = columns // parts
+
+    def project_part(ahead):
+        start = wrap(lax.div(place.z, 2) + ahead, parts) * size
+        project(pair, terms, total, start, size)
+
+    first = parts // 2
+    others = sorted((k for k in range(parts) if k != first), key=lambda k: (-min(k, parts - k), k))
+    events_part = [(0.05, functools.partial(project_part, k)) for k in others]
 
     def chain():
-        yield from gram_steps(place, mail, left, both, part, z_in, y_in, gram, lambda: project(pair, left, total))
+        yield from gram_steps(place, mail, left, both, part, z_in, y_in, gram, lambda: project_part(first))
         for c in range(2):
             a[:, c * half : (c + 1) * half] = gram[c]
         yield from factor_steps(a, w)
@@ -550,7 +573,7 @@
         ortho[...] = exact_dot(both[0, own, :], w[:, :half], 1, 1) + exact_dot(both[1, own, :], w[:, half:], 1, 1)
         yield 1.0
 
-    merge(chain(), events_y + events_z)
+    merge(chain(), events_y + events_z + events_part)
 
     own = pl.ds(pl.multiple_of(place.chip() * piece, 8), piece)
     i = mail.take(1)
@@ -619,6 +642,7 @@
     half = rank // 2
     piece = 2 * shard
     long = 128 if piece == 208 else 32
+    sum_long = SUM_LONG if piece == 208 else 32
     chips = nz * ny
     across = rank // nx
     ring = 2 * chips + nz + ny
@@ -642,9 +666,9 @@
             vmem((2, 2 * rows, half), F32), vmem((across, half), F32),
             vmem((nz, across // nz, half), F32), vmem((ny, across // nz, half), F32),
             vmem((2, rank, half), F32), vmem((rank, rank), F32), vmem((rank, rank), F32),
-            vmem((columns, half), F32),
-            vmem((chips, long, half), F32), vmem((nz, long, half), F32),
-            vmem((chips, piece - long, half), F32), vmem((ny, piece - long, half), F32),
+            vmem((columns, half), F32), vmem((2 * rows, rank), BF16),
+            vmem((chips, sum_long, half), F32), vmem((nz, sum_long, half), F32),
+            vmem((chips, piece - sum_long, half), F32), vmem((ny, piece - sum_long, half), F32),
             vmem((2, piece, half), F32), vmem((rows, rank), F32),
             vmem((nz, 8, rank), F32), vmem((ny, 8, rank), F32), vmem((nx, 8, rank), F32),
             dma((2,)), dma((ring,)), dma((ring,)), dma((ring,)), dma((ring,)), dma((ring,)), dma((ring,)),
@@ -673,7 +697,7 @@
 def apply_call(step, momentum, gradient, stacked, gathered):
     rows, columns = momentum.shape
     rank = stacked.shape[1]
-    width = 512 if columns % 512 == 0 else BLOCK
+    width = columns // 2 if columns % 256 == 0 else BLOCK
     tile = pl.BlockSpec((rows, width), lambda i: (0, i))
     return pl.pallas_call(
         functools.partial(apply_kernel, step),

time: 173 us -> 173 us (level)
    pallas_call x1, Pallas kernels: 159 us -> 165 us  [step_call(): pl.pallas_call(functools.partial(step_kernel, dims, magnitude), out_shape...]
    pallas_call x1, Pallas kernels: 12.5 us -> 7.12 us  [apply_call(): pl.pallas_call(functools.partial(apply_kernel, step), grid=(columns // wi...]
where the time goes in v3:
time: 173 us
  Pallas kernels  172 us (99%)
    pallas_call x1, Pallas kernels, step_call(): pl.pallas_call(functools.partial(step_kernel, dims, magnitude), out_shape...  165 us
    pallas_call x1, Pallas kernels, apply_call(): pl.pallas_call(functools.partial(apply_kernel, step), grid=(columns // wi...  7.12 us

profile of v3, /device:TPU:1, one launch (start us, length us, event | category | flops | bytes accessed | tf_op | source)
XLA Modules:
  0.0 173.2 jit_solution(13793524298587778563)
XLA Ops:
  0.6 164.8 %dion_step.1 = (bf16[2,6656,256]{2,1,0:T(8,128)(2,1)}, bf16[256,512]{1,0:T(8,128)(2,1)}, bf16[104,512]{1,0:T(8,128)(2,1)}) custom-call(f32[128,6656]{1,0:T(8,128)} %momentum.3, bf16[128,6656]{1,0:T(8,128)(2,1)} %gradient.3, bf16[104,512]{1,0:T(8,128)(2,1)} %bitcast.3), custom_call_target="tpu_custom_call" | custom-call | tf_op jit(solution)/shard_map/dion_step/pallas_call | solution.py:652
  165.4 0.0 copy-start
  165.4 7.1 %apply.1 = (f32[128,6656]{1,0:T(8,128)}, bf16[128,6656]{1,0:T(8,128)(2,1)}) custom-call(f32[128,6656]{1,0:T(8,128)} %momentum.3, bf16[128,6656]{1,0:T(8,128)(2,1)} %gradient.3, bf16[256,512]{1,0:T(8,128)(2,1)} %get-tuple-element.8.stacked, bf16[2,6656,256]{2,1,0:T(8,128)(2,1)} %get-tuple-element.9.gathered), custom_call_target="tpu_custom_call" | custom-call | tf_op jit(solution)/shard_map/apply/pallas_call | solution.py:702
  172.5 0.0 copy-done
  172.5 0.6 copy.7
Async XLA Ops:
  165.4 7.1 %copy-start = (bf16[104,512]{1,0:T(8,128)(2,1)S(1)}, bf16[104,512]{1,0:T(8,128)(2,1)}, u32[]{:S(2)}) copy-start(bf16[104,512]{1,0:T(8,128)(2,1)} %get-tuple-element.12) | copy-start | bytes 319492

commit v4 on v3

--- a/solution.py
+++ b/solution.py
@@ -9,7 +9,7 @@
 from jax.sharding import PartitionSpec as P
 
 PER_Y, HOP_Y, PER_Z, HOP_Z = 4.5, 4.5, 9.0, 4.0
-GRAM_TIMES = (0.0, 3.5, 5.0, 5.5, 1.5)
+GRAM_TIMES = (1.0, 4.5, 6.0, 7.5, 3.0)
 FACTOR_SCALE = 1.0
 SUM_LONG = 128
 WHEN = {0: 0.0, 1: 1.0, 2: 1.4, 3: 2.4, 4: 2.8}
@@ -463,17 +463,20 @@
 def project(pair, terms, total, begin, size):
     rows = pair.shape[1]
     half = total.shape[1]
-    width = next(w for w in (832, 512, 384, BLOCK) if size % w == 0 and w % BLOCK == 0)
-
-    @pl.loop(0, size // width)
-    def _(i):
-        at = pl.ds(pl.multiple_of(begin + i * width, BLOCK), width)
+    width = 512 if size >= 512 else BLOCK
+
+    def block(start, width):
+        at = pl.ds(pl.multiple_of(start, BLOCK), width)
         value = sum(
             lax.dot_general(pair[c, :, at], terms[c * rows : (c + 1) * rows, :], (((0,), (0,)), ((), ())),
                             preferred_element_type=F32)
             for c in range(2)
         )
         total[at, :] = value[:, :half] + value[:, half:]
+
+    pl.loop(0, size // width)(lambda i: block(begin + i * width, width))
+    if size % width:
+        block(begin + size // width * width, size % width)
 
 
 def merge(steps, events, begin=0.0):

time: 173 us -> 165 us (0.954)
  Pallas kernels: 172 us -> 164 us
    pallas_call x1, Pallas kernels: 165 us -> 157 us  [step_call(): pl.pallas_call(functools.partial(step_kernel, dims, magnitude), out_shape...]
where the time goes in v4:
time: 165 us
  Pallas kernels  164 us (99%)
    pallas_call x1, Pallas kernels, step_call(): pl.pallas_call(functools.partial(step_kernel, dims, magnitude), out_shape...  157 us
    pallas_call x1, Pallas kernels, apply_call(): pl.pallas_call(functools.partial(apply_kernel, step), grid=(columns // wi...  7.12 us

profile of v4, /device:TPU:1, one launch (start us, length us, event | category | flops | bytes accessed | tf_op | source)
XLA Modules:
  0.0 165.2 jit_solution(2913384879042634398)
XLA Ops:
  0.6 156.7 %dion_step.1 = (bf16[2,6656,256]{2,1,0:T(8,128)(2,1)}, bf16[256,512]{1,0:T(8,128)(2,1)}, bf16[104,512]{1,0:T(8,128)(2,1)}) custom-call(f32[128,6656]{1,0:T(8,128)} %momentum.3, bf16[128,6656]{1,0:T(8,128)(2,1)} %gradient.3, bf16[104,512]{1,0:T(8,128)(2,1)} %bitcast.3), custom_call_target="tpu_custom_call" | custom-call | tf_op jit(solution)/shard_map/dion_step/pallas_call | solution.py:655
  157.4 0.0 copy-start
  157.4 7.1 %apply.1 = (f32[128,6656]{1,0:T(8,128)}, bf16[128,6656]{1,0:T(8,128)(2,1)}) custom-call(f32[128,6656]{1,0:T(8,128)} %momentum.3, bf16[128,6656]{1,0:T(8,128)(2,1)} %gradient.3, bf16[256,512]{1,0:T(8,128)(2,1)} %get-tuple-element.8.stacked, bf16[2,6656,256]{2,1,0:T(8,128)(2,1)} %get-tuple-element.9.gathered), custom_call_target="tpu_custom_call" | custom-call | tf_op jit(solution)/shard_map/apply/pallas_call | solution.py:705
  164.5 0.0 copy-done
  164.5 0.6 copy.7
Async XLA Ops:
  157.4 7.1 %copy-start = (bf16[104,512]{1,0:T(8,128)(2,1)S(1)}, bf16[104,512]{1,0:T(8,128)(2,1)}, u32[]{:S(2)}) copy-start(bf16[104,512]{1,0:T(8,128)(2,1)} %get-tuple-element.12) | copy-start | bytes 319492
